TPU v7x, 128 devices: a whole 4x4x4 slice. The times are simulated.
128 devices in a mesh: seq: 16 (over z_hi, x, core), head: 8 (over z_lo, y).
Axes of the slice: x: 4, y: 4, z: 4 (z_hi: 2, z_lo: 2; z = z_hi * 2 + z_lo), core: 2. Of those that a mesh axis runs over, the one named last changes fastest.
Arguments:
- queries: bfloat16 [65536, 512], P('seq'), may hold values from -250 to 250
- memory: bfloat16 [2048, 1024], replicated, may hold values from -6 to 6
- w_query: bfloat16 [512, 512], P(None, 'head'), may hold values from -0.25 to 0.25
- w_key: bfloat16 [1024, 512], P(None, 'head'), may hold values from -0.1875 to 0.1875
- w_value: bfloat16 [1024, 512], P(None, 'head'), may hold values from -0.1875 to 0.1875
- w_out: bfloat16 [512, 512], P('head'), may hold values from -0.25 to 0.25
- grad_out: bfloat16 [65536, 512], P('seq'), may hold values from -384 to 384
- masked: int32 [65536], P('seq'), may hold values from 0 to 1, as said below
Outputs:
- grad_wq: float32 [512, 512], P('seq', 'head')
- grad_wk: float32 [1024, 512], P('seq', 'head')
- grad_wv: float32 [1024, 512], P('seq', 'head')
- grad_wo: float32 [512, 512], P('head', 'seq')
- grad_memory: float32 [2048, 1024], P('seq', 'head')
Inputs may be any that keep to these rules, and one draw needn't show every extreme that they name: The first position of every block of 4096 bytes is masked.
All inputs are finite; a program needn't handle non-finite values.
Results may differ from a plain program's by a relative error of at most 0.033.
Values sent between devices are 32-bit elements; how exact they have to be, the bound alone decides.
No kernel may reach another device: no remote copies, remote signals or barrier semaphores. Data moves between devices by JAX's collectives and lax.ppermute only.
A program may use at most 64 MiB of HBM per device.

v0:
```python
import jax
import jax.numpy as jnp
from jax import lax
from jax.sharding import PartitionSpec as P

DH = 64


def shards(queries, memory, w_query, w_key, w_value, w_out, grad_out, masked):
    f32 = jnp.float32
    bf16 = jnp.bfloat16
    mask_total = lax.psum(jnp.sum(masked).astype(f32), "seq")
    row_count, width = queries.shape
    latents, channels = memory.shape
    heads_width = w_query.shape[1]
    head_count = heads_width // DH
    seq_size = lax.axis_size("seq")
    seq_index = lax.axis_index("seq")
    latent_rows = latents // seq_size
    channel_cols = channels // seq_size
    weighted = grad_out * masked[:, None].astype(bf16)
    key_proj = (
        jnp.dot(memory, w_key, preferred_element_type=f32)
        .astype(bf16)
        .reshape(latents, head_count, DH)
    )
    value_proj = (
        jnp.dot(memory, w_value, preferred_element_type=f32)
        .astype(bf16)
        .reshape(latents, head_count, DH)
    )
    block_rows = 512
    block_count = row_count // block_rows

    def fold_block(carried, inputs_pair):
        acc_key, acc_value, acc_query, acc_out = carried
        tokens, grads = inputs_pair
        query_three = (
            jnp.dot(tokens, w_query, preferred_element_type=f32)
            .astype(bf16)
            .reshape(block_rows, head_count, DH)
        )
        score_block = (
            jnp.einsum("qhd,khd->hqk", query_three, key_proj, preferred_element_type=f32) * 0.125
        )
        top_score = jnp.max(score_block, axis=-1, keepdims=True)
        expo_block = jnp.exp(score_block - top_score)
        prob_block = expo_block / jnp.sum(expo_block, axis=-1, keepdims=True)
        prob_b = prob_block.astype(bf16)
        attended = jnp.einsum(
            "hqk,khd->qhd", prob_b, value_proj, preferred_element_type=f32
        ).astype(bf16)
        flat_att = attended.reshape(block_rows, heads_width)
        d_attended = jnp.einsum("qe,fe->qf", grads, w_out, preferred_element_type=f32).astype(bf16)
        acc_out = acc_out + jnp.einsum("qf,qe->fe", flat_att, grads, preferred_element_type=f32)
        d_three = d_attended.reshape(block_rows, head_count, DH)
        d_prob = jnp.einsum("qhd,khd->hqk", d_three, value_proj, preferred_element_type=f32)
        row_delta = jnp.einsum("qhd,qhd->hq", d_three.astype(f32), attended.astype(f32))
        d_score = (prob_block * (d_prob - row_delta[:, :, None]) * 0.125).astype(bf16)
        d_query = (
            jnp.einsum("hqk,khd->qhd", d_score, key_proj, preferred_element_type=f32)
            .astype(bf16)
            .reshape(block_rows, heads_width)
        )
        acc_query = acc_query + jnp.einsum("qe,qf->ef", tokens, d_query, preferred_element_type=f32)
        acc_key = acc_key + jnp.einsum(
            "hqk,qhd->hdk", d_score, query_three, preferred_element_type=f32
        )
        acc_value = acc_value + jnp.einsum(
            "hqk,qhd->hdk", prob_b, d_three, preferred_element_type=f32
        )
        return ((acc_key, acc_value, acc_query, acc_out), None)

    start = (
        jnp.zeros((head_count, DH, latents), f32),
        jnp.zeros((head_count, DH, latents), f32),
        jnp.zeros((width, heads_width), f32),
        jnp.zeros((heads_width, width), f32),
    )
    pairs = (
        queries.reshape(block_count, block_rows, width),
        weighted.reshape(block_count, block_rows, width),
    )
    (acc_key, acc_value, acc_query, acc_out), _ = lax.scan(fold_block, start, pairs)
    sum_key = acc_key.reshape(heads_width, latents)
    sum_value = acc_value.reshape(heads_width, latents)
    latent_start = seq_index * latent_rows
    total_key, total_value = lax.psum((sum_key, sum_value), "seq")
    full_key = (total_key / mask_total).astype(bf16)
    full_value = (total_value / mask_total).astype(bf16)
    whole_key = jnp.dot(full_key, memory, preferred_element_type=f32)
    whole_value = jnp.dot(full_value, memory, preferred_element_type=f32)
    slab_key = lax.dynamic_slice_in_dim(whole_key, seq_index * channel_cols, channel_cols, 1)
    slab_value = lax.dynamic_slice_in_dim(whole_value, seq_index * channel_cols, channel_cols, 1)
    key_rows = lax.dynamic_slice_in_dim(full_key, latent_start, latent_rows, 1)
    value_rows = lax.dynamic_slice_in_dim(full_value, latent_start, latent_rows, 1)
    memory_part = jnp.einsum("hl,ch->lc", key_rows, w_key, preferred_element_type=f32)
    memory_part = memory_part + jnp.einsum(
        "hl,ch->lc", value_rows, w_value, preferred_element_type=f32
    )
    grad_memory = lax.psum_scatter(memory_part, "head", scatter_dimension=1, tiled=True)
    share_query, share_out = (
        lax.psum_scatter(acc_query, "seq", scatter_dimension=0, tiled=True),
        lax.psum_scatter(acc_out, "seq", scatter_dimension=1, tiled=True),
    )
    grad_wq = share_query / mask_total
    grad_wo = share_out / mask_total
    return (grad_wq, slab_key.T, slab_value.T, grad_wo, grad_memory)


def solution(mesh):
    return jax.shard_map(
        shards,
        mesh=mesh,
        in_specs=(
            P("seq", None),
            P(),
            P(None, "head"),
            P(None, "head"),
            P(None, "head"),
            P("head", None),
            P("seq", None),
            P("seq"),
        ),
        out_specs=(
            P("seq", "head"),
            P("seq", "head"),
            P("seq", "head"),
            P("head", "seq"),
            P("seq", "head"),
        ),
        check_vma=False,
    )
```

profile of v0, /device:TPU:0, one launch (start us, length us, event | category | flops | bytes accessed | tf_op | source)
XLA Modules:
  0.0 485.8 jit_solution(16174864673192921703)
XLA Ops:
  7.3 1.5 fusion.34
  8.8 3.6 fusion.27
  13.8 3.9 broadcast_multiply_fusion
  17.7 140.2 %while.17 = (s32[]{:T(128)}, f32[1,64,2048]{2,1,0:T(8,128)S(1)}, f32[1,64,2048]{2,1,0:T(8,128)}, f32[512,64]{0,1:T(8,128)}, f32[64,512]{1,0:T(8,128)}, /*index=5...) while((s32[]{:T(128)}, f32[1,64,2048]{2,1,0:T(8,128)S(1)}, ...), condition=%wide.region_3.0_spmd.clone, body=%wide.region_0.3_spmd.clone.sunk | while | flops 955120128 | bytes 75710656 | solution.py:84
  21.5 2.0 copy-done.1
  25.6 3.7 fusion.100
  30.6 2.7 fusion.101
  33.2 1.9 convolution_add_fusion.3
  38.9 2.0 copy-done.1
  43.0 3.8 fusion.100
  48.1 2.7 fusion.101
  50.8 1.9 convolution_add_fusion.3
  56.5 2.0 copy-done.1
  60.5 3.8 fusion.100
  65.6 2.7 fusion.101
  68.3 1.9 convolution_add_fusion.3
  74.0 2.0 copy-done.1
  78.1 3.8 fusion.100
  83.2 2.7 fusion.101
  85.9 1.9 convolution_add_fusion.3
  91.6 2.0 copy-done.1
  95.6 3.8 fusion.100
  100.7 2.7 fusion.101
  103.4 1.9 convolution_add_fusion.3
  109.1 2.0 copy-done.1
  113.2 3.8 fusion.100
  118.3 2.7 fusion.101
  121.0 1.9 convolution_add_fusion.3
  126.7 2.0 copy-done.1
  130.7 3.8 fusion.100
  135.8 2.7 fusion.101
  138.5 1.9 convolution_add_fusion.3
  144.2 2.0 copy-done.1
  148.3 3.8 fusion.100
  153.4 2.7 fusion.101
  156.1 1.9 convolution_add_fusion.3
  158.0 1.9 copy.20
  160.7 1.7 copy.19
  163.2 39.3 %psum.21 = f32[]{:T(128)} all-reduce(f32[]{:T(128)S(6)} %convert_element_type.50), channel_id=1, replica_groups=mesh['seq'=16,'head'=8] {'seq'}, use_global_device_ids=true, to_apply=%region_6.7 | all-reduce | flops 1 | bytes 8 | tf_op jit(solution)/shard_map/psum | solution.py:12
  202.5 25.1 %reduce-scatter.6.cloned.1.call-done = f32[64,32]{0,1:T(8,128)} async-done(((f32[64,512]{0,1:T(8,128)}), f32[64,32]{0,1:T(8,128)}) %reduce-scatter.6.cloned.1.call-update) | async-done | bytes 8208 | tf_op jit(solution)/shard_map/reduce_scatter | solution.py:104
  227.6 2.0 broadcast_divide_fusion
  229.5 140.4 %all-reduce.3.cloned.1.call-done = (f32[64,2048]{1,0:T(8,128)}, f32[64,2048]{1,0:T(8,128)}) async-done(((f32[64,2048]{1,0:T(8,128)}, f32[64,2048]{1,0:T(8,128)}), (f32[64,2048]{1,0:T(8,128)}, f32[64,2048]{1,0:T(8,128)})) %all-reduce.3.cloned.1.call-update) | async-done | bytes 1048592 | tf_op jit(solution)/shard_map/psum | solution.py:88
  369.9 1.9 divide_convert_fusion
  373.2 66.3 %reduce-scatter.4.cloned.1.call-done = f32[32,64]{1,0:T(8,128)} async-done(((f32[512,64]{1,0:T(8,128)}), f32[32,64]{1,0:T(8,128)}) %reduce-scatter.4.cloned.1.call-update) | async-done | bytes 8208 | tf_op jit(solution)/shard_map/reduce_scatter | solution.py:103
  439.5 2.0 broadcast_divide_fusion.1
  441.5 3.0 fusion.36
  445.3 3.0 fusion.35
  449.2 30.1 %reduce-scatter.8.cloned.1.call-done = f32[128,128]{1,0:T(8,128)} async-done(((f32[128,1024]{1,0:T(8,128)}), f32[128,128]{1,0:T(8,128)}) %reduce-scatter.8.cloned.1.call-update) | async-done | bytes 65552 | tf_op jit(solution)/shard_map/reduce_scatter | solution.py:101
  (119 shorter events, 62.5 us)
Async XLA Ops:
  7.2 1.6 copy-start
  7.2 5.2 %copy-start.6 = (bf16[1024,64]{0,1:T(8,128)(2,1)S(1)}, bf16[1024,64]{0,1:T(8,128)(2,1)}, u32[]{:S(2)}) copy-start(bf16[1024,64]{0,1:T(8,128)(2,1)} %param.14) | copy-start | bytes 393220
  7.2 220.4 %reduce-scatter.6.cloned.1.call-start = ((), (), s32[]{:S(2)}) async-start(), calls=%async_computation.4 | async-start | bytes 278528 | tf_op jit(solution)/shard_map/reduce_scatter | solution.py:104
  7.3 5.1 %copy-start.3 = (bf16[2048,1024]{1,0:T(8,128)(2,1)S(1)}, bf16[2048,1024]{1,0:T(8,128)(2,1)}, u32[]{:S(2)}) copy-start(bf16[2048,1024]{1,0:T(8,128)(2,1)} %param.11) | copy-start | bytes 12582916
  13.8 3.9 copy-start.5
  21.5 2.0 copy-start.1
  25.6 3.7 copy-start.2
  38.9 2.0 copy-start.1
  43.0 3.8 copy-start.2
  56.4 2.0 copy-start.1
  60.5 3.8 copy-start.2
  74.0 2.0 copy-start.1
  78.1 3.8 copy-start.2
  91.5 2.0 copy-start.1
  95.6 3.8 copy-start.2
  109.1 2.0 copy-start.1
  113.2 3.8 copy-start.2
  126.6 2.0 copy-start.1
  130.7 3.8 copy-start.2
  144.2 2.0 copy-start.1
  148.3 3.8 copy-start.2
  158.0 2.0 copy-start.4
  158.0 214.2 %copy-start.7 = (bf16[1024,64]{0,1:T(8,128)(2,1)S(1)}, bf16[1024,64]{0,1:T(8,128)(2,1)}, u32[]{:S(2)}) copy-start(bf16[1024,64]{0,1:T(8,128)(2,1)} %param.14) | copy-start | bytes 393220
  159.9 210.0 %all-reduce.3.cloned.1.call-start = ((), (), s32[]{:S(2)}) async-start(), calls=%async_computation.6 | async-start | bytes 2097152 | tf_op jit(solution)/shard_map/psum | solution.py:88
  160.7 278.9 %reduce-scatter.4.cloned.1.call-start = ((), (), s32[]{:S(2)}) async-start(), calls=%async_computation.3 | async-start | bytes 278528 | tf_op jit(solution)/shard_map/reduce_scatter | solution.py:103
  162.5 316.8 %reduce-scatter.8.cloned.1.call-start = ((), (), s32[]{:S(2)}) async-start(), calls=%async_computation.5 | async-start | bytes 589824 | tf_op jit(solution)/shard_map/reduce_scatter | solution.py:101
Sparse Core Ops, SparseCore 0:
  160.0 67.4 reduce-scatter.5
  230.2 139.6 all-reduce.2
  373.7 65.8 reduce-scatter.3
  442.5 36.7 reduce-scatter.7
where the time goes:
time: 487 us; the launch traced here: 486 us
  waiting for transfers between devices  263 us (54%)
  matrix products  123 us (25%)
  blocking collectives  39.3 us (8%)
  other arithmetic  24.3 us (5%)
  local copies, waits for them, and re-layouts  21 us (4%)
  between operations  14.5 us (3%)
    psum x1, waiting for transfers between devices, shards(): total_key, total_value = lax.psum((sum_key, sum_value), 'seq')  140 us
    reduce_scatter x1, waiting for transfers between devices, shards(): lax.psum_scatter(acc_query, 'seq', scatter_dimension=0, tiled=True)  66.3 us
    psum x1, blocking collectives, shards(): mask_total = lax.psum(jnp.sum(masked).astype(f32), 'seq')  39.3 us
    dot_general x8, matrix products, fold_block(): jnp.einsum('hqk,qhd->hdk', prob_b, d_three, preferred_element_type=f32)  30.2 us
    reduce_scatter x1, waiting for transfers between devices, shards(): lax.psum_scatter(memory_part, 'head', scatter_dimension=1, tiled=True)  30.1 us
    reduce_scatter x1, waiting for transfers between devices, shards(): lax.psum_scatter(acc_out, 'seq', scatter_dimension=1, tiled=True)  25.1 us
    dot_general x8, matrix products, fold_block(): jnp.einsum('qe,qf->ef', tokens, d_query, preferred_element_type=f32)  21.4 us
    while x32, local copies, waits for them, and re-layouts  15.7 us
  transfers between devices with their start and end apart: 4, of which 4 were waited for; matrix products, arithmetic and copies ran while one was open for 3% of the time, Pallas kernels for 0%

commit v1 on v0

v1 whole, which is shorter than its diff:
```python
import functools

import jax
import jax.numpy as jnp
from jax import lax
from jax.experimental import pallas as pl
from jax.experimental.pallas import tpu as pltpu
from jax.sharding import PartitionSpec as P

DH = 64
ROWS = 4096
LAT = 2048
E = 512
C = 1024
PACK = 256
SMALL = 128
LARGE = 272
TB = 256
MEM_PARTS = 4
ROW_PARTS = 4
f32 = jnp.float32
bf16 = jnp.bfloat16


def _dot(a, b, dims):
    return lax.dot_general(a, b, (dims, ((), ())), preferred_element_type=f32)


NN = ((1,), (0,))
NT = ((1,), (1,))


def main_kernel(
    sidx, masked, q_hbm, g_hbm, mem_hbm, wq_hbm, wk_hbm, wv_hbm, wo_hbm,
    keep_a, send_a, keep_b, send_b,
    q_in, g_in, mem, wq, wk, wv, wo, qc, gc, kv, wkv, wq2, wo2, pos, off_v, off_s,
    dkv, wqo, wkv_out, wqo_out,
    mem_sem, row_sem, w_sem, off_sem,
):
    me = sidx[0]
    w_copies = [
        pltpu.make_async_copy(src, dst, w_sem.at[i])
        for i, (src, dst) in enumerate(((wk_hbm, wk), (wv_hbm, wv), (wq_hbm, wq), (wo_hbm, wo)))
    ]
    mrows = LAT // MEM_PARTS
    mem_copies = [
        pltpu.make_async_copy(
            mem_hbm.at[pl.ds(i * mrows, mrows)], mem.at[pl.ds(i * mrows, mrows)], mem_sem.at[i]
        )
        for i in range(MEM_PARTS)
    ]
    rrows = ROWS // ROW_PARTS
    row_copies = [
        [
            pltpu.make_async_copy(
                src.at[pl.ds(i * rrows, rrows)], dst.at[pl.ds(i * rrows, rrows)], row_sem.at[2 * i + j]
            )
            for j, (src, dst) in enumerate(((q_hbm, q_in), (g_hbm, g_in)))
        ]
        for i in range(ROW_PARTS)
    ]
    for c in w_copies + mem_copies:
        c.start()
    for pair in row_copies:
        for c in pair:
            c.start()

    ones = masked[...].astype(f32)
    mb = ones.astype(bf16)
    r128 = lax.broadcasted_iota(jnp.int32, (128, 128), 0)
    c128 = lax.broadcasted_iota(jnp.int32, (128, 128), 1)
    before = (r128 < c128).astype(f32).astype(bf16)
    rank = _dot(mb, before, NN)
    counts = _dot(mb, jnp.ones((128, 128), bf16), NN)
    r40 = lax.broadcasted_iota(jnp.int32, (40, 32), 0)
    c40 = lax.broadcasted_iota(jnp.int32, (40, 32), 1)
    earlier = (c40 < r40).astype(f32).astype(bf16)
    offs = _dot(earlier, counts.astype(bf16), NN)
    off_v[...] = offs.astype(jnp.int32)
    off_copy = pltpu.make_async_copy(off_v, off_s, off_sem)
    off_copy.start()
    pos[...] = jnp.where(ones > 0.5, offs[:32] + rank, -1.0).astype(jnp.int32)

    dkv[...] = jnp.zeros_like(dkv)
    wqo[...] = jnp.zeros_like(wqo)
    qc[pl.ds(0, 16), :] = jnp.zeros((16, E), bf16)
    gc[pl.ds(0, 16), :] = jnp.zeros((16, E), bf16)

    for c in w_copies:
        c.wait()
    wkv[:, :DH] = wk[...]
    wkv[:, DH:] = wv[...]
    wq2[:, :DH] = wq[...]
    wq2[:, DH:] = jnp.zeros((E, DH), bf16)
    wo2[:DH, :] = jnp.zeros((DH, E), bf16)
    wo2[DH:, :] = wo[...]
    for i, c in enumerate(mem_copies):
        c.wait()
        part = pl.ds(i * mrows, mrows)
        kv[part, :] = _dot(mem[part, :], wkv[...], NN).astype(bf16)

    off_copy.wait()
    total = off_s[32, 0]

    def put(b, start, size):
        row = lax.broadcasted_iota(jnp.int32, (size, 128), 0) + start
        picks = [
            (row == pos[pl.ds(2 * b + half, 1), :]).astype(f32).astype(bf16) for half in range(2)
        ]
        pick = jnp.concatenate(picks, axis=1)
        src = pl.ds(b * PACK, PACK)
        first = pl.ds(start, 16)
        rest = pl.ds(pl.multiple_of(start + 16, 16), size - 16)
        for s_ref, d_ref in ((q_in, qc), (g_in, gc)):
            rows = _dot(pick, s_ref[src, :], NN)
            d_ref[first, :] = (rows[:16] + d_ref[first, :].astype(f32)).astype(bf16)
            d_ref[rest, :] = rows[16:].astype(bf16)

    per = rrows // PACK
    for b in range(ROWS // PACK):
        if b % per == 0:
            for c in row_copies[b // per]:
                c.wait()
        base = off_s[2 * b, 0]
        nxt = off_s[2 * b + 2, 0]
        start = pl.multiple_of((base // 16) * 16, 16)
        few = nxt - start < SMALL
        pl.when(few)(functools.partial(put, b, start, SMALL))
        pl.when(jnp.logical_not(few))(functools.partial(put, b, start, LARGE))

    tail = pl.ds(pl.multiple_of(((total + 15) // 16) * 16, 16), TB)
    qc[tail, :] = jnp.zeros((TB, E), bf16)
    gc[tail, :] = jnp.zeros((TB, E), bf16)

    def block(i, _):
        rows = pl.ds(pl.multiple_of(i * TB, TB), TB)
        q = qc[rows, :]
        g = gc[rows, :]
        qp = _dot(q, wq2[...], NN).astype(bf16).astype(f32) * 0.125
        da = _dot(g, wo2[...], NT).astype(bf16)
        score = _dot(qp.astype(bf16), kv[...], NT)
        dprob = _dot(da, kv[...], NT)
        top = jnp.max(score, axis=1, keepdims=True)
        e = jnp.exp(score - top)
        inv = 1.0 / jnp.sum(e, axis=1, keepdims=True)
        eb = e.astype(bf16)
        att = (_dot(eb, kv[...], NN) * inv).astype(bf16)
        daf = da.astype(f32)
        delta = jnp.sum(daf * att.astype(f32), axis=1, keepdims=True)
        ds = (e * (dprob - delta)).astype(bf16)
        dq = _dot(ds, kv[...], NN) * (inv * 0.125)
        lane = lax.broadcasted_iota(jnp.int32, (TB, 128), 1)
        x = jnp.where(lane < DH, dq, att.astype(f32))
        y = (qp + daf) * inv
        xt = x.T.astype(bf16)
        yt = y.T.astype(bf16)
        wqo[:DH, :] += _dot(xt[:DH], q, NN)
        wqo[DH:, :] += _dot(xt[DH:], g, NN)
        dkv[:DH, :] += _dot(yt[:DH], ds, NN)
        dkv[DH:, :] += _dot(yt[DH:], eb, NN)
        return 0

    lax.fori_loop(0, (total + TB - 1) // TB, block, 0)

    wkvt = _dot(dkv[...].astype(bf16), mem[...], NN)
    lane64 = lax.broadcasted_iota(jnp.int32, (64, 128), 1)
    for t in range(8):
        tk = wkvt[:DH, 128 * t : 128 * (t + 1)]
        tv = wkvt[DH:, 128 * t : 128 * (t + 1)]
        wkv_out[2 * t] = jnp.where(lane64 < DH, tk, pltpu.roll(tv, 64, 1))
        wkv_out[2 * t + 1] = jnp.where(lane64 < DH, pltpu.roll(tk, 64, 1), tv)
    lane32 = lax.broadcasted_iota(jnp.int32, (32, 128), 1)
    for t in range(4):
        cols = slice(128 * t, 128 * (t + 1))
        for u in range(4):
            chunk = None
            for k, lo in ((0, 0), (1, 64), (2, 32), (3, 96)):
                piece = wqo[lo : lo + 32, cols]
                shift = (32 * (k - u)) % 128
                piece = pltpu.roll(piece, shift, 1) if shift else piece
                chunk = piece if chunk is None else jnp.where(lane32 >= 32 * k, piece, chunk)
            wqo_out[4 * t + u] = chunk
    count = jnp.zeros((8, 128), f32) + total.astype(f32)
    for p in range(16):
        rc, rx, rz = p // 8, (p // 2) % 4, p % 2
        s = me ^ (rz * 8 + rx * 2 + rc)
        a = (keep_a, send_a)[rc]
        b = (keep_b, send_b)[rc]
        i = p % 8
        a[i] = dkv[:, pl.ds(pl.multiple_of(s * 128, 128), 128)]
        b[i, 0:64] = wkv_out[s]
        b[i, 64:96] = wqo_out[s]
        b[i, 96:104] = count


def run_main(sidx, masked, queries, grads, memory, w_query, w_key, w_value, w_out):
    any_ = pl.BlockSpec(memory_space=pl.ANY)
    vm = pl.BlockSpec(memory_space=pltpu.VMEM)
    a = jax.ShapeDtypeStruct((8, 128, 128), f32)
    b = jax.ShapeDtypeStruct((8, 104, 128), f32)
    pad = ROWS + LARGE + TB
    return pl.pallas_call(
        main_kernel,
        out_shape=(a, a, b, b),
        in_specs=[pl.BlockSpec(memory_space=pltpu.SMEM), vm] + [any_] * 7,
        out_specs=(vm,) * 4,
        scratch_shapes=[
            pltpu.VMEM((ROWS, E), bf16),
            pltpu.VMEM((ROWS, E), bf16),
            pltpu.VMEM((LAT, C), bf16),
            pltpu.VMEM((E, DH), bf16),
            pltpu.VMEM((C, DH), bf16),
            pltpu.VMEM((C, DH), bf16),
            pltpu.VMEM((DH, E), bf16),
            pltpu.VMEM((pad, E), bf16),
            pltpu.VMEM((pad, E), bf16),
            pltpu.VMEM((LAT, 128), bf16),
            pltpu.VMEM((C, 128), bf16),
            pltpu.VMEM((E, 128), bf16),
            pltpu.VMEM((128, E), bf16),
            pltpu.VMEM((32, 128), jnp.int32),
            pltpu.VMEM((40, 128), jnp.int32),
            pltpu.SMEM((40, 128), jnp.int32),
            pltpu.VMEM((128, LAT), f32),
            pltpu.VMEM((128, E), f32),
            pltpu.VMEM((16, 64, 128), f32),
            pltpu.VMEM((16, 32, 128), f32),
            pltpu.SemaphoreType.DMA((MEM_PARTS,)),
            pltpu.SemaphoreType.DMA((2 * ROW_PARTS,)),
            pltpu.SemaphoreType.DMA((4,)),
            pltpu.SemaphoreType.DMA(()),
        ],
        compiler_params=pltpu.CompilerParams(vmem_limit_bytes=60 * 1024 * 1024),
        cost_estimate=pl.CostEstimate(flops=10**10, bytes_accessed=14 * 2**20, transcendentals=10**7),
        name="masked_rows",
    )(sidx, masked, queries, grads, memory, w_query, w_key, w_value, w_out)


def head_kernel(hidx, part0, part1, wk, wv, keep_al, send_al, keep_be, send_be):
    me = hidx[0]
    d = (part0[...] + part1[...]).astype(bf16)
    dt = d.T
    for ry in range(4):
        for rz in range(2):
            c = me ^ (rz * 4 + ry)
            rows = pl.ds(pl.multiple_of(c * 128, 128), 128)
            w = jnp.concatenate([wk[rows, :], wv[rows, :]], axis=1)
            out = _dot(dt, w, NT)
            al = (keep_al, 0) if ry == 0 else (keep_al, 1) if ry == 3 else (send_al, ry - 1)
            be = (keep_be, ry) if ry < 2 else (send_be, 3 - ry)
            al[0][al[1], rz] = out[:64]
            be[0][be[1], rz] = out[64:]


def run_head(hidx, part0, part1, w_key, w_value):
    vm = pl.BlockSpec(memory_space=pltpu.VMEM)
    o = jax.ShapeDtypeStruct((2, 2, 64, 128), f32)
    return pl.pallas_call(
        head_kernel,
        out_shape=(o,) * 4,
        in_specs=[pl.BlockSpec(memory_space=pltpu.SMEM)] + [vm] * 4,
        out_specs=(vm,) * 4,
        name="memory_part",
    )(hidx, part0, part1, w_key, w_value)


def swap(x, axis, bits):
    n = lax.axis_size(axis)
    return lax.ppermute(x, axis, [(i, i ^ bits) for i in range(n)])


def ring_reduce(al_keep, al_send, be_keep, be_send, axis, near, far):
    al_in = swap(al_send, axis, near)
    be_in = swap(be_send, axis, far)
    al1_send = al_keep[1] + al_in[1]
    be1_send = be_keep[1] + be_in[1]
    al1_in = swap(al1_send, axis, far)
    be1_in = swap(be1_send, axis, near)
    al1 = al_keep[0] + al_in[0]
    be1 = be_keep[0] + be_in[0]
    return al1 + al1_in, be1 + be1_in


def shards(queries, memory, w_query, w_key, w_value, w_out, grad_out, masked):
    seq = lax.axis_index("seq").astype(jnp.int32).reshape(1)
    head = lax.axis_index("head").astype(jnp.int32).reshape(1)
    keep_a, send_a, keep_b, send_b = run_main(
        seq, masked.reshape(32, 128), queries, grad_out, memory, w_query, w_key, w_value, w_out
    )
    in_a = swap(send_a, "seq", 1)
    in_b = swap(send_b, "seq", 1)

    def over_x(keep, got, cut):
        keep = keep.reshape(4, 2, *keep.shape[1:])
        got = got.reshape(4, 2, *got.shape[1:])
        pair = lambda i, j, lo, hi: jnp.stack(
            [keep[i, :, lo:hi] + got[i, :, lo:hi], keep[j, :, lo:hi] + got[j, :, lo:hi]]
        )
        top = keep.shape[2]
        return ring_reduce(
            pair(0, 3, 0, cut), pair(1, 2, 0, cut), pair(0, 1, cut, top), pair(3, 2, cut, top),
            "seq", 2, 6,
        )

    al, be = over_x(keep_a, in_a, 64)
    send = jnp.concatenate([al[1], be[1]], axis=0)
    got = swap(send, "seq", 8)
    mine = jnp.concatenate([al[0], be[0]], axis=0)
    keep_al, send_al, keep_be, send_be = run_head(head, mine, got, w_key, w_value)

    bl, bh = over_x(keep_b, in_b, 56)
    send = jnp.concatenate([bl[1], bh[1]], axis=0)
    b = jnp.concatenate([bl[0], bh[0]], axis=0) + swap(send, "seq", 8)
    total = b[96:97, 0:1]

    ml, mh = ring_reduce(keep_al, send_al, keep_be, send_be, "head", 1, 3)
    mem = jnp.concatenate([ml, mh], axis=1)
    grad_memory = (mem[0] + swap(mem[1], "head", 4)) / total

    b = b / total
    grad_wk = b[0:64, 0:64].T
    grad_wv = b[0:64, 64:128].T
    rest = b[64:96]
    grad_wq = jnp.concatenate([rest[:, 0:32], rest[:, 64:96]], axis=0).T
    grad_wo = jnp.concatenate([rest[:, 32:64], rest[:, 96:128]], axis=0)
    return (grad_wq, grad_wk, grad_wv, grad_wo, grad_memory)


def solution(mesh):
    return jax.shard_map(
        shards,
        mesh=mesh,
        in_specs=(
            P("seq", None),
            P(),
            P(None, "head"),
            P(None, "head"),
            P(None, "head"),
            P("head", None),
            P("seq", None),
            P("seq"),
        ),
        out_specs=(
            P("seq", "head"),
            P("seq", "head"),
            P("seq", "head"),
            P("head", "seq"),
            P("seq", "head"),
        ),
        check_vma=False,
    )
```

time: 487 us -> 100 us (0.21)
  waiting for transfers between devices: 263 us -> 23.8 us
  matrix products: 123 us -> 0 us
  blocking collectives: 39.3 us -> 0 us
  starting transfers between devices: 0.16 us -> 30.8 us
  Pallas kernels: 0 us -> 21 us
  between operations: 14.5 us -> 0.79 us
  local copies, waits for them, and re-layouts: 21 us -> 9.22 us
  other arithmetic: 24.3 us -> 13.8 us
    psum x1 -> x0, waiting for transfers between devices: 140 us -> none  [shards(): total_key, total_value = lax.psum((sum_key, sum_value), 'seq')]
    dot_general x78 -> x0, matrix products: 123 us -> none  [the longest x8 30.2 us: fold_block(): jnp.einsum('hqk,qhd->hdk', prob_b, d_three, preferred_element_type=f32)]
    reduce_scatter x3 -> x0, waiting for transfers between devices: 121 us -> none  [the longest x1 66.3 us: shards(): lax.psum_scatter(acc_query, 'seq', scatter_dimension=0, tiled=True)]
    psum x1 -> x0, blocking collectives: 39.3 us -> none  [shards(): mask_total = lax.psum(jnp.sum(masked).astype(f32), 'seq')]
    ppermute x0 -> x17, starting transfers between devices: none -> 30.8 us  [swap(): return lax.ppermute(x, axis, [(i, i ^ bits) for i in range(n)])]
    ppermute x0 -> x17, waiting for transfers between devices: none -> 23.8 us  [swap(): return lax.ppermute(x, axis, [(i, i ^ bits) for i in range(n)])]
    pallas_call x0 -> x2, Pallas kernels: none -> 21 us  [the longest x1 18.7 us: run_main(): pl.pallas_call(main_kernel, out_shape=(a, a, b, b), in_specs=[pl.BlockSpe...]
    while x34 -> x0, local copies, waits for them, and re-layouts: 19.4 us -> none
  transfers between devices with their start and end apart: 4 -> 17, of which waited for: 4 -> 11; matrix products, arithmetic and copies ran while one was open for 3% -> 13% of each run, Pallas kernels for 0% -> 0%
where the time goes in v1:
time: 100 us; the launch traced here: 99.5 us
  starting transfers between devices  30.8 us (31%)
  waiting for transfers between devices  23.8 us (24%)
  Pallas kernels  21 us (21%)
  other arithmetic  13.8 us (14%)
  local copies, waits for them, and re-layouts  9.22 us (9%)
    ppermute x17, starting transfers between devices, swap(): return lax.ppermute(x, axis, [(i, i ^ bits) for i in range(n)])  30.8 us
    ppermute x17, waiting for transfers between devices, swap(): return lax.ppermute(x, axis, [(i, i ^ bits) for i in range(n)])  23.8 us
    pallas_call x1, Pallas kernels, run_main(): pl.pallas_call(main_kernel, out_shape=(a, a, b, b), in_specs=[pl.BlockSpe...  18.7 us
    unnamed x9, local copies, waits for them, and re-layouts  8.47 us
    add x5, other arithmetic, ring_reduce(): return (al1 + al1_in, be1 + be1_in)  4.28 us
    add x3, other arithmetic, over_x(): keep[i, :, lo:hi] + got[i, :, lo:hi]  2.69 us
    add x3, other arithmetic, ring_reduce(): al1_send = al_keep[1] + al_in[1]  2.59 us
    pallas_call x1, Pallas kernels, run_head(): pl.pallas_call(head_kernel, out_shape=(o,) * 4, in_specs=[pl.BlockSpec(me...  2.26 us
  transfers between devices with their start and end apart: 17, of which 11 were waited for; matrix products, arithmetic and copies ran while one was open for 13% of the time, Pallas kernels for 0%

profile of v1, /device:TPU:0, one launch (start us, length us, event | category | flops | bytes accessed | tf_op | source)
XLA Modules:
  0.0 99.5 jit_solution(9045259424205705163)
XLA Ops:
  0.6 1.6 %copy.34.wq_hbm = bf16[512,64]{1,0:T(8,128)(2,1)} copy(bf16[512,64]{0,1:T(8,128)(2,1)} %param.10) | data formatting | bytes 131072 | tf_op args[2]
  2.2 1.8 %copy.35.wk_hbm.wk = bf16[1024,64]{1,0:T(8,128)(2,1)} copy(bf16[1024,64]{0,1:T(8,128)(2,1)} %param.11) | data formatting | bytes 262144 | tf_op args[3]
  4.0 1.8 %copy.36.wv_hbm.wv = bf16[1024,64]{1,0:T(8,128)(2,1)} copy(bf16[1024,64]{0,1:T(8,128)(2,1)} %param.12) | data formatting | bytes 262144 | tf_op args[4]
  5.7 18.7 %masked_rows.1 = (f32[8,128,128]{2,1,0:T(8,128)}, f32[8,128,128]{2,1,0:T(8,128)}, f32[8,104,128]{2,1,0:T(8,128)}, f32[8,104,128]{2,1,0:T(8,128)}) custom-call(s32[1]{0:T(128)} %bitcast.sidx, s32[32,128]{1,0:T(8,128)} %bitcast.92, bf16[4096,512]{1,0:T(8,128)(2,1)} %q_hbm.1, bf16[4096,512]{1,0:T(8,128)(2,1)} %g_hbm.1, bf16[2048,1024]{1,0:T(8,128)(2,1)} %mem_hbm.1, ...), custom_call_target="tpu_custom_call" | custom-call | flops 10000000000 | bytes 14680064 | tf_op jit(solution)/shard_map/masked_rows/pallas_call | solution.py:202
  25.1 1.5 %collective-permute-done = f32[8,104,128]{2,1,0:T(8,128)S(1)} collective-permute-done((f32[8,104,128]{2,1,0:T(8,128)}, f32[8,104,128]{2,1,0:T(8,128)S(1)}, u32[]{:S(2)}, u32[]{:S(2)}) %collective-permute-start) | collective-permute-done | bytes 426016 | tf_op jit(solution)/shard_map/ppermute | solution.py:269
  26.5 0.8 slice_add_fusion.26
  27.4 5.3 %collective-permute-start.3 = (f32[2,2,48,128]{3,2,1,0:T(8,128)S(1)}, f32[2,2,48,128]{3,2,1,0:T(8,128)S(1)}, u32[]{:S(2)}, u32[]{:S(2)}) collective-permute-start(f32[2,2,48,128]{3,2,1,0:T(8,128)S(1)} %pad_maximum_fusion.3), channel_id=1, source_target_pairs={{0,48},{8,56},{16,32},{24,40},{32,16},{40,24},{48,0},{56,8},{64,11... | collective-permute-start | bytes 294920 | tf_op jit(solution)/shard_map/ppermute | solution.py:269
  32.7 0.9 slice_add_fusion.20
  33.9 1.9 %collective-permute-done.3 = f32[2,2,48,128]{3,2,1,0:T(8,128)S(1)} collective-permute-done((f32[2,2,48,128]{3,2,1,0:T(8,128)S(1)}, f32[2,2,48,128]{3,2,1,0:T(8,128)S(1)}, u32[]{:S(2)}, u32[]{:S(2)}) %collective-permute-start.3) | collective-permute-done | bytes 98336 | tf_op jit(solution)/shard_map/ppermute | solution.py:269
  35.8 0.8 fusion.20
  36.6 0.5 collective-permute-start.4
  37.1 1.0 slice_add_fusion.14
  38.1 2.8 %collective-permute-start.9 = (f32[2,2,64,128]{3,2,1,0:T(8,128)S(1)}, f32[2,2,64,128]{3,2,1,0:T(8,128)S(1)}, u32[]{:S(2)}, u32[]{:S(2)}) collective-permute-start(f32[2,2,64,128]{3,2,1,0:T(8,128)S(1)} %pad_maximum_fusion.1), channel_id=1, source_target_pairs={{0,48},{8,56},{16,32},{24,40},{32,16},{40,24},{48,0},{56,8},{64,11... | collective-permute-start | bytes 393224 | tf_op jit(solution)/shard_map/ppermute | solution.py:269
  40.9 0.8 fusion.17
  41.8 0.8 collective-permute-start.2
  42.6 0.8 fusion.22
  43.4 3.8 %collective-permute-done.2 = f32[2,56,128]{2,1,0:T(8,128)S(1)} collective-permute-done((f32[2,56,128]{2,1,0:T(8,128)S(1)}, f32[2,56,128]{2,1,0:T(8,128)S(1)}, u32[]{:S(2)}, u32[]{:S(2)}) %collective-permute-start.2) | collective-permute-done | bytes 57376 | tf_op jit(solution)/shard_map/ppermute | solution.py:269
  47.2 0.8 fusion.19
  48.1 8.7 %collective-permute-start.5 = (f32[104,128]{1,0:T(8,128)S(1)}, f32[104,128]{1,0:T(8,128)S(1)}, u32[]{:S(2)}, u32[]{:S(2)}) collective-permute-start(f32[104,128]{1,0:T(8,128)S(1)} %pad_maximum_fusion.7), channel_id=1, source_target_pairs={{0,64},{8,72},{16,80},{24,88},{32,96},{40,104},{48,112},{56,120},{... | collective-permute-start | bytes 159752 | tf_op jit(solution)/shard_map/ppermute | solution.py:269
  57.1 1.8 %collective-permute-done.5 = f32[104,128]{1,0:T(8,128)S(1)} collective-permute-done((f32[104,128]{1,0:T(8,128)S(1)}, f32[104,128]{1,0:T(8,128)S(1)}, u32[]{:S(2)}, u32[]{:S(2)}) %collective-permute-start.5) | collective-permute-done | bytes 53280 | tf_op jit(solution)/shard_map/ppermute | solution.py:269
  58.9 0.6 slice.289
  59.5 0.6 broadcast_divide_fusion
  60.1 1.7 %collective-permute-done.7 = f32[2,2,64,128]{3,2,1,0:T(8,128)S(1)} collective-permute-done((f32[2,2,64,128]{3,2,1,0:T(8,128)S(1)}, f32[2,2,64,128]{3,2,1,0:T(8,128)S(1)}, u32[]{:S(2)}, u32[]{:S(2)}) %collective-permute-start.7) | collective-permute-done | bytes 131104 | tf_op jit(solution)/shard_map/ppermute | solution.py:269
  61.8 0.9 fusion.14
  62.7 0.9 collective-permute-start.8
  63.7 4.6 %collective-permute-done.8 = f32[2,64,128]{2,1,0:T(8,128)S(1)} collective-permute-done((f32[2,64,128]{2,1,0:T(8,128)S(1)}, f32[2,64,128]{2,1,0:T(8,128)S(1)}, u32[]{:S(2)}, u32[]{:S(2)}) %collective-permute-start.8) | collective-permute-done | bytes 65568 | tf_op jit(solution)/shard_map/ppermute | solution.py:269
  68.3 0.9 fusion.16
  69.2 1.9 %collective-permute-start.11 = (f32[128,128]{1,0:T(8,128)S(1)}, f32[128,128]{1,0:T(8,128)S(1)}, u32[]{:S(2)}, u32[]{:S(2)}) collective-permute-start(f32[128,128]{1,0:T(8,128)S(1)} %pad_maximum_fusion.6), channel_id=1, source_target_pairs={{0,64},{8,72},{16,80},{24,88},{32,96},{40,104},{48,112},{56,120},{... | collective-permute-start | bytes 196616 | tf_op jit(solution)/shard_map/ppermute | solution.py:269
  71.2 0.6 pad_maximum_fusion.5.part0
  71.8 3.3 %collective-permute-done.11.part1 = f32[128,128]{1,0:T(8,128)S(1)} collective-permute-done((f32[128,128]{1,0:T(8,128)S(1)}, f32[128,128]{1,0:T(8,128)S(1)}, u32[]{:S(2)}, u32[]{:S(2)}) %collective-permute-start.11) | collective-permute-done | bytes 65568 | tf_op jit(solution)/shard_map/ppermute | solution.py:269
  75.1 0.6 copy-done
  75.7 2.3 %memory_part.1 = (f32[2,2,64,128]{3,2,1,0:T(8,128)}, f32[2,2,64,128]{3,2,1,0:T(8,128)}, f32[2,2,64,128]{3,2,1,0:T(8,128)}, f32[2,2,64,128]{3,2,1,0:T(8,128)}) custom-call(s32[1]{0:T(128)} %bitcast.16.hidx, f32[128,128]{1,0:T(8,128)} %pad_maximum_fusion.5.part0, f32[128,128]{1,0:T(8,128)} %copy-done, bf16[1024,64]{1,0:T(8,128)(2,1)} %copy.35.wk_hbm.wk, ...), custom_call_target="tpu_custom_call" | custom-call | tf_op jit(solution)/shard_map/memory_part/pallas_call | solution.py:258
  78.0 1.6 %collective-permute-start.12 = (f32[2,2,64,128]{3,2,1,0:T(8,128)}, f32[2,2,64,128]{3,2,1,0:T(8,128)S(1)}, u32[]{:S(2)}, u32[]{:S(2)}) collective-permute-start(f32[2,2,64,128]{3,2,1,0:T(8,128)} %get-tuple-element.18), channel_id=1, source_target_pairs={{0,1},{1,0},{2,3},{3,2},{4,5},{5,4},{6,7},{7,6},{8,9},{9,8},{10,11... | collective-permute-start | bytes 393224 | tf_op jit(solution)/shard_map/ppermute | solution.py:269
  79.6 2.2 %collective-permute-start.14 = (f32[2,2,64,128]{3,2,1,0:T(8,128)}, f32[2,2,64,128]{3,2,1,0:T(8,128)S(1)}, u32[]{:S(2)}, u32[]{:S(2)}) collective-permute-start(f32[2,2,64,128]{3,2,1,0:T(8,128)} %get-tuple-element.20), channel_id=1, source_target_pairs={{0,3},{1,2},{2,1},{3,0},{4,7},{5,6},{6,5},{7,4},{8,11},{9,10},{10,... | collective-permute-start | bytes 393224 | tf_op jit(solution)/shard_map/ppermute | solution.py:269
  81.8 1.3 %collective-permute-done.12 = f32[2,2,64,128]{3,2,1,0:T(8,128)S(1)} collective-permute-done((f32[2,2,64,128]{3,2,1,0:T(8,128)}, f32[2,2,64,128]{3,2,1,0:T(8,128)S(1)}, u32[]{:S(2)}, u32[]{:S(2)}) %collective-permute-start.12) | collective-permute-done | bytes 131104 | tf_op jit(solution)/shard_map/ppermute | solution.py:269
  83.2 0.9 fusion.8
  84.0 3.8 %collective-permute-start.13 = (f32[2,64,128]{2,1,0:T(8,128)S(1)}, f32[2,64,128]{2,1,0:T(8,128)S(1)}, u32[]{:S(2)}, u32[]{:S(2)}) collective-permute-start(f32[2,64,128]{2,1,0:T(8,128)S(1)} %fusion.8), channel_id=1, source_target_pairs={{0,3},{1,2},{2,1},{3,0},{4,7},{5,6},{6,5},{7,4},{8,11},{9,10},{10,... | collective-permute-start | bytes 196616 | tf_op jit(solution)/shard_map/ppermute | solution.py:269
  87.8 0.9 fusion.5
  88.7 1.3 %collective-permute-done.13 = f32[2,64,128]{2,1,0:T(8,128)S(1)} collective-permute-done((f32[2,64,128]{2,1,0:T(8,128)S(1)}, f32[2,64,128]{2,1,0:T(8,128)S(1)}, u32[]{:S(2)}, u32[]{:S(2)}) %collective-permute-start.13) | collective-permute-done | bytes 65568 | tf_op jit(solution)/shard_map/ppermute | solution.py:269
  90.0 0.9 fusion.10
  90.9 2.1 %collective-permute-done.15 = f32[2,64,128]{2,1,0:T(8,128)S(1)} collective-permute-done((f32[2,64,128]{2,1,0:T(8,128)S(1)}, f32[2,64,128]{2,1,0:T(8,128)S(1)}, u32[]{:S(2)}, u32[]{:S(2)}) %collective-permute-start.15) | collective-permute-done | bytes 65568 | tf_op jit(solution)/shard_map/ppermute | solution.py:269
  93.0 0.9 fusion.7
  93.9 1.1 %collective-permute-start.16 = (f32[128,128]{1,0:T(8,128)S(1)}, f32[128,128]{1,0:T(8,128)S(1)}, u32[]{:S(2)}, u32[]{:S(2)}) collective-permute-start(f32[128,128]{1,0:T(8,128)S(1)} %fusion.4), channel_id=1, source_target_pairs={{0,4},{1,5},{2,6},{3,7},{4,0},{5,1},{6,2},{7,3},{8,12},{9,13},{10,... | collective-permute-start | bytes 196616 | tf_op jit(solution)/shard_map/ppermute | solution.py:269
  95.0 0.7 copy.39
  95.6 0.7 copy.41
  96.3 0.7 copy.42
  97.0 0.7 copy.40
  98.2 1.3 %fusion.3 = f32[128,128]{1,0:T(8,128)} fusion(f32[128,128]{1,0:T(8,128)S(1)} %collective-permute-done.16, f32[2,64,128]{2,1,0:T(8,128)S(1)} %fusion.10, f32[2,64,128]{2,1,0:T(8,128)S(1)} %fusion.7, f32[]{:T(128)} %bitcast.12), kind=kLoop, calls=%fused_computation.9 | loop fusion | flops 49152 | bytes 262148 | tf_op jit(solution)/shard_map/div | solution.py:318
  (28 shorter events, 2.0 us)
Async XLA Ops:
  24.5 2.1 %collective-permute-start = (f32[8,104,128]{2,1,0:T(8,128)}, f32[8,104,128]{2,1,0:T(8,128)S(1)}, u32[]{:S(2)}, u32[]{:S(2)}) collective-permute-start(f32[8,104,128]{2,1,0:T(8,128)} %get-tuple-element.14), channel_id=1, source_target_pairs={{0,8},{8,0},{16,24},{24,16},{32,40},{40,32},{48,56},{56,48},{64,72... | collective-permute-start | bytes 1277960 | tf_op jit(solution)/shard_map/ppermute | solution.py:269
  24.6 12.6 %collective-permute-start.6 = (f32[8,128,128]{2,1,0:T(8,128)}, f32[8,128,128]{2,1,0:T(8,128)S(1)}, u32[]{:S(2)}, u32[]{:S(2)}) collective-permute-start(f32[8,128,128]{2,1,0:T(8,128)} %get-tuple-element.16), channel_id=1, source_target_pairs={{0,8},{8,0},{16,24},{24,16},{32,40},{40,32},{48,56},{56,48},{64,72... | collective-permute-start | bytes 1572872 | tf_op jit(solution)/shard_map/ppermute | solution.py:269
  27.4 8.4 %collective-permute-start.3 = (f32[2,2,48,128]{3,2,1,0:T(8,128)S(1)}, f32[2,2,48,128]{3,2,1,0:T(8,128)S(1)}, u32[]{:S(2)}, u32[]{:S(2)}) collective-permute-start(f32[2,2,48,128]{3,2,1,0:T(8,128)S(1)} %pad_maximum_fusion.3), channel_id=1, source_target_pairs={{0,48},{8,56},{16,32},{24,40},{32,16},{40,24},{48,0},{56,8},{64,11... | collective-permute-start | bytes 294920 | tf_op jit(solution)/shard_map/ppermute | solution.py:269
  33.6 7.3 %collective-permute-start.1 = (f32[2,2,56,128]{3,2,1,0:T(8,128)S(1)}, f32[2,2,56,128]{3,2,1,0:T(8,128)S(1)}, u32[]{:S(2)}, u32[]{:S(2)}) collective-permute-start(f32[2,2,56,128]{3,2,1,0:T(8,128)S(1)} %pad_maximum_fusion.2), channel_id=1, source_target_pairs={{0,16},{8,24},{16,0},{24,8},{32,48},{40,56},{48,32},{56,40},{64,80... | collective-permute-start | bytes 344072 | tf_op jit(solution)/shard_map/ppermute | solution.py:269
  36.6 6.0 %collective-permute-start.4 = (f32[2,48,128]{2,1,0:T(8,128)S(1)}, f32[2,48,128]{2,1,0:T(8,128)S(1)}, u32[]{:S(2)}, u32[]{:S(2)}) collective-permute-start(f32[2,48,128]{2,1,0:T(8,128)S(1)} %fusion.20), channel_id=1, source_target_pairs={{0,16},{8,24},{16,0},{24,8},{32,48},{40,56},{48,32},{56,40},{64,80... | collective-permute-start | bytes 147464 | tf_op jit(solution)/shard_map/ppermute | solution.py:269
  38.1 22.0 %collective-permute-start.9 = (f32[2,2,64,128]{3,2,1,0:T(8,128)S(1)}, f32[2,2,64,128]{3,2,1,0:T(8,128)S(1)}, u32[]{:S(2)}, u32[]{:S(2)}) collective-permute-start(f32[2,2,64,128]{3,2,1,0:T(8,128)S(1)} %pad_maximum_fusion.1), channel_id=1, source_target_pairs={{0,48},{8,56},{16,32},{24,40},{32,16},{40,24},{48,0},{56,8},{64,11... | collective-permute-start | bytes 393224 | tf_op jit(solution)/shard_map/ppermute | solution.py:269
  41.8 5.5 %collective-permute-start.2 = (f32[2,56,128]{2,1,0:T(8,128)S(1)}, f32[2,56,128]{2,1,0:T(8,128)S(1)}, u32[]{:S(2)}, u32[]{:S(2)}) collective-permute-start(f32[2,56,128]{2,1,0:T(8,128)S(1)} %fusion.17), channel_id=1, source_target_pairs={{0,48},{8,56},{16,32},{24,40},{32,16},{40,24},{48,0},{56,8},{64,11... | collective-permute-start | bytes 172040 | tf_op jit(solution)/shard_map/ppermute | solution.py:269
  48.1 10.8 %collective-permute-start.5 = (f32[104,128]{1,0:T(8,128)S(1)}, f32[104,128]{1,0:T(8,128)S(1)}, u32[]{:S(2)}, u32[]{:S(2)}) collective-permute-start(f32[104,128]{1,0:T(8,128)S(1)} %pad_maximum_fusion.7), channel_id=1, source_target_pairs={{0,64},{8,72},{16,80},{24,88},{32,96},{40,104},{48,112},{56,120},{... | collective-permute-start | bytes 159752 | tf_op jit(solution)/shard_map/ppermute | solution.py:269
  56.8 5.0 %collective-permute-start.7 = (f32[2,2,64,128]{3,2,1,0:T(8,128)S(1)}, f32[2,2,64,128]{3,2,1,0:T(8,128)S(1)}, u32[]{:S(2)}, u32[]{:S(2)}) collective-permute-start(f32[2,2,64,128]{3,2,1,0:T(8,128)S(1)} %pad_maximum_fusion), channel_id=1, source_target_pairs={{0,16},{8,24},{16,0},{24,8},{32,48},{40,56},{48,32},{56,40},{64,80... | collective-permute-start | bytes 393224 | tf_op jit(solution)/shard_map/ppermute | solution.py:269
  62.7 5.6 %collective-permute-start.8 = (f32[2,64,128]{2,1,0:T(8,128)S(1)}, f32[2,64,128]{2,1,0:T(8,128)S(1)}, u32[]{:S(2)}, u32[]{:S(2)}) collective-permute-start(f32[2,64,128]{2,1,0:T(8,128)S(1)} %get-tuple-element.28), channel_id=1, source_target_pairs={{0,48},{8,56},{16,32},{24,40},{32,16},{40,24},{48,0},{56,8},{64,11... | collective-permute-start | bytes 196616 | tf_op jit(solution)/shard_map/ppermute | solution.py:269
  63.7 4.6 %collective-permute-start.10 = (f32[2,64,128]{2,1,0:T(8,128)S(1)}, f32[2,64,128]{2,1,0:T(8,128)S(1)}, u32[]{:S(2)}, u32[]{:S(2)}) collective-permute-start(f32[2,64,128]{2,1,0:T(8,128)S(1)} %get-tuple-element.29), channel_id=1, source_target_pairs={{0,16},{8,24},{16,0},{24,8},{32,48},{40,56},{48,32},{56,40},{64,80... | collective-permute-start | bytes 196616 | tf_op jit(solution)/shard_map/ppermute | solution.py:269
  69.2 5.8 %collective-permute-start.11 = (f32[128,128]{1,0:T(8,128)S(1)}, f32[128,128]{1,0:T(8,128)S(1)}, u32[]{:S(2)}, u32[]{:S(2)}) collective-permute-start(f32[128,128]{1,0:T(8,128)S(1)} %pad_maximum_fusion.6), channel_id=1, source_target_pairs={{0,64},{8,72},{16,80},{24,88},{32,96},{40,104},{48,112},{56,120},{... | collective-permute-start | bytes 196616 | tf_op jit(solution)/shard_map/ppermute | solution.py:269
  75.1 0.6 copy-start
  78.0 5.2 %collective-permute-start.12 = (f32[2,2,64,128]{3,2,1,0:T(8,128)}, f32[2,2,64,128]{3,2,1,0:T(8,128)S(1)}, u32[]{:S(2)}, u32[]{:S(2)}) collective-permute-start(f32[2,2,64,128]{3,2,1,0:T(8,128)} %get-tuple-element.18), channel_id=1, source_target_pairs={{0,1},{1,0},{2,3},{3,2},{4,5},{5,4},{6,7},{7,6},{8,9},{9,8},{10,11... | collective-permute-start | bytes 393224 | tf_op jit(solution)/shard_map/ppermute | solution.py:269
  79.6 8.2 %collective-permute-start.14 = (f32[2,2,64,128]{3,2,1,0:T(8,128)}, f32[2,2,64,128]{3,2,1,0:T(8,128)S(1)}, u32[]{:S(2)}, u32[]{:S(2)}) collective-permute-start(f32[2,2,64,128]{3,2,1,0:T(8,128)} %get-tuple-element.20), channel_id=1, source_target_pairs={{0,3},{1,2},{2,1},{3,0},{4,7},{5,6},{6,5},{7,4},{8,11},{9,10},{10,... | collective-permute-start | bytes 393224 | tf_op jit(solution)/shard_map/ppermute | solution.py:269
  84.0 6.0 %collective-permute-start.13 = (f32[2,64,128]{2,1,0:T(8,128)S(1)}, f32[2,64,128]{2,1,0:T(8,128)S(1)}, u32[]{:S(2)}, u32[]{:S(2)}) collective-permute-start(f32[2,64,128]{2,1,0:T(8,128)S(1)} %fusion.8), channel_id=1, source_target_pairs={{0,3},{1,2},{2,1},{3,0},{4,7},{5,6},{6,5},{7,4},{8,11},{9,10},{10,... | collective-permute-start | bytes 196616 | tf_op jit(solution)/shard_map/ppermute | solution.py:269
  88.6 4.3 %collective-permute-start.15 = (f32[2,64,128]{2,1,0:T(8,128)S(1)}, f32[2,64,128]{2,1,0:T(8,128)S(1)}, u32[]{:S(2)}, u32[]{:S(2)}) collective-permute-start(f32[2,64,128]{2,1,0:T(8,128)S(1)} %fusion.5), channel_id=1, source_target_pairs={{0,1},{1,0},{2,3},{3,2},{4,5},{5,4},{6,7},{7,6},{8,9},{9,8},{10,11... | collective-permute-start | bytes 196616 | tf_op jit(solution)/shard_map/ppermute | solution.py:269
  93.9 4.3 %collective-permute-start.16 = (f32[128,128]{1,0:T(8,128)S(1)}, f32[128,128]{1,0:T(8,128)S(1)}, u32[]{:S(2)}, u32[]{:S(2)}) collective-permute-start(f32[128,128]{1,0:T(8,128)S(1)} %fusion.4), channel_id=1, source_target_pairs={{0,4},{1,5},{2,6},{3,7},{4,0},{5,1},{6,2},{7,3},{8,12},{9,13},{10,... | collective-permute-start | bytes 196616 | tf_op jit(solution)/shard_map/ppermute | solution.py:269

commit v2 on v1

--- a/solution.py
+++ b/solution.py
@@ -33,14 +33,21 @@
 def main_kernel(
     sidx, masked, q_hbm, g_hbm, mem_hbm, wq_hbm, wk_hbm, wv_hbm, wo_hbm,
     keep_a, send_a, keep_b, send_b,
-    q_in, g_in, mem, wq, wk, wv, wo, qc, gc, kv, wkv, wq2, wo2, pos, off_v, off_s,
+    q_in, g_in, mem, qc, gc, kv, wkv, wq2, wo2, pos, off_v, off_s,
     dkv, wqo, wkv_out, wqo_out,
     mem_sem, row_sem, w_sem, off_sem,
 ):
     me = sidx[0]
     w_copies = [
         pltpu.make_async_copy(src, dst, w_sem.at[i])
-        for i, (src, dst) in enumerate(((wk_hbm, wk), (wv_hbm, wv), (wq_hbm, wq), (wo_hbm, wo)))
+        for i, (src, dst) in enumerate(
+            (
+                (wk_hbm, wkv.at[pl.ds(0, DH)]),
+                (wv_hbm, wkv.at[pl.ds(DH, DH)]),
+                (wq_hbm, wq2.at[pl.ds(0, DH)]),
+                (wo_hbm, wo2.at[pl.ds(DH, DH)]),
+            )
+        )
     ]
     mrows = LAT // MEM_PARTS
     mem_copies = [
@@ -88,16 +95,12 @@
 
     for c in w_copies:
         c.wait()
-    wkv[:, :DH] = wk[...]
-    wkv[:, DH:] = wv[...]
-    wq2[:, :DH] = wq[...]
-    wq2[:, DH:] = jnp.zeros((E, DH), bf16)
+    wq2[DH:, :] = jnp.zeros((DH, E), bf16)
     wo2[:DH, :] = jnp.zeros((DH, E), bf16)
-    wo2[DH:, :] = wo[...]
     for i, c in enumerate(mem_copies):
         c.wait()
         part = pl.ds(i * mrows, mrows)
-        kv[part, :] = _dot(mem[part, :], wkv[...], NN).astype(bf16)
+        kv[part, :] = _dot(mem[part, :], wkv[...], NT).astype(bf16)
 
     off_copy.wait()
     total = off_s[32, 0]
@@ -136,7 +139,7 @@
         rows = pl.ds(pl.multiple_of(i * TB, TB), TB)
         q = qc[rows, :]
         g = gc[rows, :]
-        qp = _dot(q, wq2[...], NN).astype(bf16).astype(f32) * 0.125
+        qp = _dot(q, wq2[...], NT).astype(bf16).astype(f32) * 0.125
         da = _dot(g, wo2[...], NT).astype(bf16)
         score = _dot(qp.astype(bf16), kv[...], NT)
         dprob = _dot(da, kv[...], NT)
@@ -208,15 +211,11 @@
             pltpu.VMEM((ROWS, E), bf16),
             pltpu.VMEM((ROWS, E), bf16),
             pltpu.VMEM((LAT, C), bf16),
-            pltpu.VMEM((E, DH), bf16),
-            pltpu.VMEM((C, DH), bf16),
-            pltpu.VMEM((C, DH), bf16),
-            pltpu.VMEM((DH, E), bf16),
             pltpu.VMEM((pad, E), bf16),
             pltpu.VMEM((pad, E), bf16),
             pltpu.VMEM((LAT, 128), bf16),
-            pltpu.VMEM((C, 128), bf16),
-            pltpu.VMEM((E, 128), bf16),
+            pltpu.VMEM((128, C), bf16),
+            pltpu.VMEM((128, E), bf16),
             pltpu.VMEM((128, E), bf16),
             pltpu.VMEM((32, 128), jnp.int32),
             pltpu.VMEM((40, 128), jnp.int32),
@@ -230,7 +229,7 @@
             pltpu.SemaphoreType.DMA((4,)),
             pltpu.SemaphoreType.DMA(()),
         ],
-        compiler_params=pltpu.CompilerParams(vmem_limit_bytes=60 * 1024 * 1024),
+        compiler_params=pltpu.CompilerParams(vmem_limit_bytes=48 * 1024 * 1024),
         cost_estimate=pl.CostEstimate(flops=10**10, bytes_accessed=14 * 2**20, transcendentals=10**7),
         name="masked_rows",
     )(sidx, masked, queries, grads, memory, w_query, w_key, w_value, w_out)
@@ -238,21 +237,20 @@
 
 def head_kernel(hidx, part0, part1, wk, wv, keep_al, send_al, keep_be, send_be):
     me = hidx[0]
-    d = (part0[...] + part1[...]).astype(bf16)
-    dt = d.T
+    dt = (part0[...] + part1[...]).T.astype(bf16)
     for ry in range(4):
         for rz in range(2):
             c = me ^ (rz * 4 + ry)
-            rows = pl.ds(pl.multiple_of(c * 128, 128), 128)
-            w = jnp.concatenate([wk[rows, :], wv[rows, :]], axis=1)
-            out = _dot(dt, w, NT)
+            cols = pl.ds(pl.multiple_of(c * 128, 128), 128)
+            w = jnp.concatenate([wk[:, cols], wv[:, cols]], axis=0)
+            out = _dot(dt, w, NN)
             al = (keep_al, 0) if ry == 0 else (keep_al, 1) if ry == 3 else (send_al, ry - 1)
             be = (keep_be, ry) if ry < 2 else (send_be, 3 - ry)
             al[0][al[1], rz] = out[:64]
             be[0][be[1], rz] = out[64:]
 
 
-def run_head(hidx, part0, part1, w_key, w_value):
+def run_head(hidx, part0, part1, wk_t, wv_t):
     vm = pl.BlockSpec(memory_space=pltpu.VMEM)
     o = jax.ShapeDtypeStruct((2, 2, 64, 128), f32)
     return pl.pallas_call(
@@ -261,7 +259,33 @@
         in_specs=[pl.BlockSpec(memory_space=pltpu.SMEM)] + [vm] * 4,
         out_specs=(vm,) * 4,
         name="memory_part",
-    )(hidx, part0, part1, w_key, w_value)
+    )(hidx, part0, part1, wk_t, wv_t)
+
+
+def weights_kernel(part0, part1, gwq, gwk, gwv, gwo_t, total):
+    b = part0[...] + part1[...]
+    count = b[96:104, :]
+    total[...] = count
+    b = b / count[0:1, :]
+    kv_t = b[0:64].T
+    gwk[...] = kv_t[:64]
+    gwv[...] = kv_t[64:]
+    qo_t = b[64:96].T
+    gwq[...] = jnp.concatenate([qo_t[0:32], qo_t[64:96]], axis=1)
+    gwo_t[...] = jnp.concatenate([qo_t[32:64], qo_t[96:128]], axis=1)
+
+
+def run_weights(part0, part1):
+    vm = pl.BlockSpec(memory_space=pltpu.VMEM)
+    small = jax.ShapeDtypeStruct((32, 64), f32)
+    square = jax.ShapeDtypeStruct((64, 64), f32)
+    return pl.pallas_call(
+        weights_kernel,
+        out_shape=(small, square, square, small, jax.ShapeDtypeStruct((8, 128), f32)),
+        in_specs=[vm] * 2,
+        out_specs=(vm,) * 5,
+        name="weight_parts",
+    )(part0, part1)
 
 
 def swap(x, axis, bits):
@@ -269,61 +293,66 @@
     return lax.ppermute(x, axis, [(i, i ^ bits) for i in range(n)])
 
 
-def ring_reduce(al_keep, al_send, be_keep, be_send, axis, near, far):
-    al_in = swap(al_send, axis, near)
-    be_in = swap(be_send, axis, far)
-    al1_send = al_keep[1] + al_in[1]
-    be1_send = be_keep[1] + be_in[1]
-    al1_in = swap(al1_send, axis, far)
-    be1_in = swap(be1_send, axis, near)
-    al1 = al_keep[0] + al_in[0]
-    be1 = be_keep[0] + be_in[0]
-    return al1 + al1_in, be1 + be1_in
+hold = lax.optimization_barrier
 
 
 def shards(queries, memory, w_query, w_key, w_value, w_out, grad_out, masked):
     seq = lax.axis_index("seq").astype(jnp.int32).reshape(1)
     head = lax.axis_index("head").astype(jnp.int32).reshape(1)
+    wk_t, wv_t = w_key.T, w_value.T
     keep_a, send_a, keep_b, send_b = run_main(
-        seq, masked.reshape(32, 128), queries, grad_out, memory, w_query, w_key, w_value, w_out
+        seq, masked.reshape(32, 128), queries, grad_out, memory, w_query.T, wk_t, wv_t, w_out
     )
-    in_a = swap(send_a, "seq", 1)
-    in_b = swap(send_b, "seq", 1)
-
-    def over_x(keep, got, cut):
-        keep = keep.reshape(4, 2, *keep.shape[1:])
-        got = got.reshape(4, 2, *got.shape[1:])
-        pair = lambda i, j, lo, hi: jnp.stack(
-            [keep[i, :, lo:hi] + got[i, :, lo:hi], keep[j, :, lo:hi] + got[j, :, lo:hi]]
-        )
-        top = keep.shape[2]
-        return ring_reduce(
-            pair(0, 3, 0, cut), pair(1, 2, 0, cut), pair(0, 1, cut, top), pair(3, 2, cut, top),
-            "seq", 2, 6,
-        )
-
-    al, be = over_x(keep_a, in_a, 64)
-    send = jnp.concatenate([al[1], be[1]], axis=0)
+    got_a = swap(send_a, "seq", 1)
+    sum_a = hold(keep_a + got_a).reshape(4, 2, 128, 128)
+    al_send, be_send = sum_a[1:3, :, :64], jnp.stack([sum_a[3, :, 64:], sum_a[2, :, 64:]])
+    al_send, be_send, send_b = hold((al_send, be_send, send_b))
+    al_in = swap(al_send, "seq", 2)
+    be_in = swap(be_send, "seq", 6)
+    got_b = swap(send_b, "seq", 1)
+    al_in, be_in, got_b = hold((al_in, be_in, got_b))
+
+    al_send, be_send = hold((sum_a[3, :, :64] + al_in[1], sum_a[1, :, 64:] + be_in[1]))
+    al_in2 = swap(al_send, "seq", 6)
+    be_in2 = swap(be_send, "seq", 2)
+    sum_b = hold(keep_b + got_b).reshape(4, 2, 104, 128)
+    bl_send, bh_send = sum_b[1:3, :, :56], jnp.stack([sum_b[3, :, 56:], sum_b[2, :, 56:]])
+    al = sum_a[0, :, :64] + al_in[0] + al_in2
+    be = sum_a[0, :, 64:] + be_in[0] + be_in2
+    sums = jnp.concatenate([al, be], axis=1)
+    mine, send, bl_send, bh_send = hold((sums[0], sums[1], bl_send, bh_send))
     got = swap(send, "seq", 8)
-    mine = jnp.concatenate([al[0], be[0]], axis=0)
-    keep_al, send_al, keep_be, send_be = run_head(head, mine, got, w_key, w_value)
-
-    bl, bh = over_x(keep_b, in_b, 56)
-    send = jnp.concatenate([bl[1], bh[1]], axis=0)
-    b = jnp.concatenate([bl[0], bh[0]], axis=0) + swap(send, "seq", 8)
-    total = b[96:97, 0:1]
-
-    ml, mh = ring_reduce(keep_al, send_al, keep_be, send_be, "head", 1, 3)
+    bl_in = swap(bl_send, "seq", 2)
+    bh_in = swap(bh_send, "seq", 6)
+    got, bl_in, bh_in = hold((got, bl_in, bh_in))
+
+    keep_al, send_al, keep_be, send_be = run_head(head, mine, got, wk_t, wv_t)
+    bl_send, bh_send = sum_b[3, :, :56] + bl_in[1], sum_b[1, :, 56:] + bh_in[1]
+    send_al, send_be, bl_send, bh_send = hold((send_al, send_be, bl_send, bh_send))
+    ml_in = swap(send_al, "head", 1)
+    mh_in = swap(send_be, "head", 3)
+    bl_in2 = swap(bl_send, "seq", 6)
+    bh_in2 = swap(bh_send, "seq", 2)
+    ml_in, mh_in, bl_in2, bh_in2 = hold((ml_in, mh_in, bl_in2, bh_in2))
+
+    ml_send, mh_send = keep_al[1] + ml_in[1], keep_be[1] + mh_in[1]
+    bl = sum_b[0, :, :56] + bl_in[0] + bl_in2
+    bh = sum_b[0, :, 56:] + bh_in[0] + bh_in2
+    sums = jnp.concatenate([bl, bh], axis=1)
+    ml_send, mh_send, mine_b, send_b = hold((ml_send, mh_send, sums[0], sums[1]))
+    ml_in2 = swap(ml_send, "head", 3)
+    mh_in2 = swap(mh_send, "head", 1)
+    got_b = swap(send_b, "seq", 8)
+    ml_in2, mh_in2, got_b = hold((ml_in2, mh_in2, got_b))
+
+    ml = keep_al[0] + ml_in[0] + ml_in2
+    mh = keep_be[0] + mh_in[0] + mh_in2
     mem = jnp.concatenate([ml, mh], axis=1)
-    grad_memory = (mem[0] + swap(mem[1], "head", 4)) / total
-
-    b = b / total
-    grad_wk = b[0:64, 0:64].T
-    grad_wv = b[0:64, 64:128].T
-    rest = b[64:96]
-    grad_wq = jnp.concatenate([rest[:, 0:32], rest[:, 64:96]], axis=0).T
-    grad_wo = jnp.concatenate([rest[:, 32:64], rest[:, 96:128]], axis=0)
-    return (grad_wq, grad_wk, grad_wv, grad_wo, grad_memory)
+    mine, send = hold((mem[0], mem[1]))
+    got = swap(send, "head", 4)
+    grad_wq, grad_wk, grad_wv, grad_wo_t, total = run_weights(mine_b, got_b)
+    grad_memory = (mine + got) / total[0:1, :]
+    return (grad_wq, grad_wk, grad_wv, grad_wo_t.T, grad_memory)
 
 
 def solution(mesh):

time: 100 us -> 81.5 us (0.81)
  other arithmetic: 13.8 us -> 4.75 us
  waiting for transfers between devices: 23.8 us -> 19.2 us
  local copies, waits for them, and re-layouts: 9.22 us -> 5.49 us
  Pallas kernels: 21 us -> 19.4 us
    add x14 -> x11, other arithmetic: 11.2 us -> 2.81 us  [the longest x2 1.7 us: shards(): ml_send, mh_send = (keep_al[1] + ml_in[1], keep_be[1] + mh_in[1])]
    ppermute x17, waiting for transfers between devices: 23.8 us -> 19.2 us  [swap(): return lax.ppermute(x, axis, [(i, i ^ bits) for i in range(n)])]
    unnamed x9 -> x14, local copies, waits for them, and re-layouts: 8.47 us -> 4.78 us
    pallas_call x1, Pallas kernels: 18.7 us -> 15.6 us  [run_main(): pl.pallas_call(main_kernel, out_shape=(a, a, b, b), in_specs=[pl.BlockSpe...]
    pallas_call x0 -> x1, Pallas kernels: none -> 1.63 us  [run_weights(): pl.pallas_call(weights_kernel, out_shape=(small, square, square, small, j...]
    squeeze x1 -> x3, other arithmetic: 0.01 us -> 1.28 us  [the longest x1 0.64 us: shards(): mine, send, bl_send, bh_send = hold((sums[0], sums[1], bl_send, bh_send))]
    div x2 -> x1, other arithmetic: 1.91 us -> 0.64 us  [shards(): grad_memory = (mine + got) / total[0:1, :]]
  transfers between devices with their start and end apart: 17 -> 17, of which waited for: 11 -> 9; matrix products, arithmetic and copies ran while one was open for 13% -> 1% of each run, Pallas kernels for 0% -> 2%
where the time goes in v2:
time: 81.5 us; the launch traced here: 80.3 us
  starting transfers between devices  30.6 us (38%)
  Pallas kernels  19.4 us (24%)
  waiting for transfers between devices  19.2 us (24%)
  local copies, waits for them, and re-layouts  5.49 us (7%)
  other arithmetic  4.75 us (6%)
    ppermute x17, starting transfers between devices, swap(): return lax.ppermute(x, axis, [(i, i ^ bits) for i in range(n)])  30.6 us
    ppermute x17, waiting for transfers between devices, swap(): return lax.ppermute(x, axis, [(i, i ^ bits) for i in range(n)])  19.2 us
    pallas_call x1, Pallas kernels, run_main(): pl.pallas_call(main_kernel, out_shape=(a, a, b, b), in_specs=[pl.BlockSpe...  15.6 us
    unnamed x14, local copies, waits for them, and re-layouts  4.78 us
    pallas_call x1, Pallas kernels, run_head(): pl.pallas_call(head_kernel, out_shape=(o,) * 4, in_specs=[pl.BlockSpec(me...  2.11 us
    add x2, other arithmetic, shards(): ml_send, mh_send = (keep_al[1] + ml_in[1], keep_be[1] + mh_in[1])  1.7 us
  transfers between devices with their start and end apart: 17, of which 9 were waited for; matrix products, arithmetic and copies ran while one was open for 1% of the time, Pallas kernels for 2%

profile of v2, /device:TPU:0, one launch (start us, length us, event | category | flops | bytes accessed | tf_op | source)
XLA Modules:
  0.0 80.3 jit_solution(12745461011050492637)
XLA Ops:
  0.6 0.0 copy-start
  0.7 0.9 %copy-done = bf16[1024,64]{0,1:T(8,128)(2,1)S(1)} copy-done((bf16[1024,64]{0,1:T(8,128)(2,1)S(1)}, bf16[1024,64]{0,1:T(8,128)(2,1)}, u32[]{:S(2)}) %copy-start) | copy-done | bytes 131096
  1.5 0.9 %copy-done.1 = bf16[1024,64]{0,1:T(8,128)(2,1)S(1)} copy-done((bf16[1024,64]{0,1:T(8,128)(2,1)S(1)}, bf16[1024,64]{0,1:T(8,128)(2,1)}, u32[]{:S(2)}) %copy-start.1) | copy-done | bytes 131096
  2.5 0.8 %copy-done.2 = bf16[512,64]{0,1:T(8,128)(2,1)S(1)} copy-done((bf16[512,64]{0,1:T(8,128)(2,1)S(1)}, bf16[512,64]{0,1:T(8,128)(2,1)}, u32[]{:S(2)}) %copy-start.2) | copy-done | bytes 65560
  3.3 0.8 %copy-done.3 = bf16[64,512]{1,0:T(8,128)(2,1)S(1)} copy-done((bf16[64,512]{1,0:T(8,128)(2,1)S(1)}, bf16[64,512]{1,0:T(8,128)(2,1)}, u32[]{:S(2)}) %copy-start.3) | copy-done | bytes 65560
  4.1 0.7 copy-done.4
  4.8 15.6 %masked_rows.1 = (f32[8,128,128]{2,1,0:T(8,128)S(1)}, f32[8,128,128]{2,1,0:T(8,128)S(1)}, f32[8,104,128]{2,1,0:T(8,128)S(1)}, f32[8,104,128]{2,1,0:T(8,128)S(1)}) custom-call(s32[1]{0:T(128)} %bitcast.1.sidx, s32[32,128]{1,0:T(8,128)S(1)} %bitcast.60, bf16[4096,512]{1,0:T(8,128)(2,1)} %q_hbm.1, bf16[4096,512]{1,0:T(8,128)(2,1)} %g_hbm.1, ...), custom_call_target="tpu_custom_call" | custom-call | flops 10000000000 | bytes 14680064 | tf_op jit(solution)/shard_map/masked_rows/pallas_call | solution.py:205
  20.5 0.1 collective-permute-start
  20.6 1.9 %collective-permute-done = f32[8,128,128]{2,1,0:T(8,128)S(1)} collective-permute-done((f32[8,128,128]{2,1,0:T(8,128)S(1)}, f32[8,128,128]{2,1,0:T(8,128)S(1)}, u32[]{:S(2)}, u32[]{:S(2)}) %collective-permute-start) | collective-permute-done | bytes 524320 | tf_op jit(solution)/shard_map/ppermute | solution.py:293
  22.5 0.1 add.99
  22.6 0.2 collective-permute-start.3
  22.8 4.0 %collective-permute-start.1 = (f32[2,2,64,128]{3,2,1,0:T(8,128)S(1)}, f32[2,2,64,128]{3,2,1,0:T(8,128)S(1)}, u32[]{:S(2)}, u32[]{:S(2)}) collective-permute-start(f32[2,2,64,128]{3,2,1,0:T(8,128)S(1)} %slice.149), channel_id=1, source_target_pairs={{0,16},{8,24},{16,0},{24,8},{32,48},{40,56},{48,32},{56,40},{64,80... | collective-permute-start | bytes 393224 | tf_op jit(solution)/shard_map/ppermute | solution.py:293
  26.8 3.7 %collective-permute-start.2 = (f32[2,2,64,128]{3,2,1,0:T(8,128)S(1)}, f32[2,2,64,128]{3,2,1,0:T(8,128)S(1)}, u32[]{:S(2)}, u32[]{:S(2)}) collective-permute-start(f32[2,2,64,128]{3,2,1,0:T(8,128)S(1)} %pad_maximum_fusion), channel_id=1, source_target_pairs={{0,48},{8,56},{16,32},{24,40},{32,16},{40,24},{48,0},{56,8},{64,11... | collective-permute-start | bytes 393224 | tf_op jit(solution)/shard_map/ppermute | solution.py:293
  30.5 0.3 collective-permute-done.1
  30.8 3.7 %collective-permute-done.2 = f32[2,2,64,128]{3,2,1,0:T(8,128)S(1)} collective-permute-done((f32[2,2,64,128]{3,2,1,0:T(8,128)S(1)}, f32[2,2,64,128]{3,2,1,0:T(8,128)S(1)}, u32[]{:S(2)}, u32[]{:S(2)}) %collective-permute-start.2) | collective-permute-done | bytes 131104 | tf_op jit(solution)/shard_map/ppermute | solution.py:293
  34.5 0.0 collective-permute-done.3
  34.6 3.0 %collective-permute-start.4 = (f32[2,64,128]{2,1,0:T(8,128)S(1)}, f32[2,64,128]{2,1,0:T(8,128)S(1)}, u32[]{:S(2)}, u32[]{:S(2)}) collective-permute-start(f32[2,64,128]{2,1,0:T(8,128)S(1)} %get-tuple-element.58), channel_id=1, source_target_pairs={{0,48},{8,56},{16,32},{24,40},{32,16},{40,24},{48,0},{56,8},{64,11... | collective-permute-start | bytes 196616 | tf_op jit(solution)/shard_map/ppermute | solution.py:293
  37.6 0.0 collective-permute-start.5
  37.6 2.5 %collective-permute-done.4 = f32[2,64,128]{2,1,0:T(8,128)S(1)} collective-permute-done((f32[2,64,128]{2,1,0:T(8,128)S(1)}, f32[2,64,128]{2,1,0:T(8,128)S(1)}, u32[]{:S(2)}, u32[]{:S(2)}) %collective-permute-start.4) | collective-permute-done | bytes 65568 | tf_op jit(solution)/shard_map/ppermute | solution.py:293
  40.2 1.7 %collective-permute-done.5 = f32[2,64,128]{2,1,0:T(8,128)S(1)} collective-permute-done((f32[2,64,128]{2,1,0:T(8,128)S(1)}, f32[2,64,128]{2,1,0:T(8,128)S(1)}, u32[]{:S(2)}, u32[]{:S(2)}) %collective-permute-start.5) | collective-permute-done | bytes 65568 | tf_op jit(solution)/shard_map/ppermute | solution.py:293
  41.9 0.6 fusion.5
  42.6 0.0 collective-permute-start.7
  42.6 1.2 %collective-permute-start.8 = (f32[2,2,48,128]{3,2,1,0:T(8,128)S(1)}, f32[2,2,48,128]{3,2,1,0:T(8,128)S(1)}, u32[]{:S(2)}, u32[]{:S(2)}) collective-permute-start(f32[2,2,48,128]{3,2,1,0:T(8,128)S(1)} %pad_maximum_fusion.1), channel_id=1, source_target_pairs={{0,48},{8,56},{16,32},{24,40},{32,16},{40,24},{48,0},{56,8},{64,11... | collective-permute-start | bytes 294920 | tf_op jit(solution)/shard_map/ppermute | solution.py:293
  43.8 6.3 %collective-permute-start.6 = (f32[128,128]{1,0:T(8,128)S(1)}, f32[128,128]{1,0:T(8,128)S(1)}, u32[]{:S(2)}, u32[]{:S(2)}) collective-permute-start(f32[128,128]{1,0:T(8,128)S(1)} %get-tuple-element.63), channel_id=1, source_target_pairs={{0,64},{8,72},{16,80},{24,88},{32,96},{40,104},{48,112},{56,120},{... | collective-permute-start | bytes 196616 | tf_op jit(solution)/shard_map/ppermute | solution.py:293
  50.1 2.2 %collective-permute-done.6.part1 = f32[128,128]{1,0:T(8,128)S(1)} collective-permute-done((f32[128,128]{1,0:T(8,128)S(1)}, f32[128,128]{1,0:T(8,128)S(1)}, u32[]{:S(2)}, u32[]{:S(2)}) %collective-permute-start.6) | collective-permute-done | bytes 65568 | tf_op jit(solution)/shard_map/ppermute | solution.py:293
  52.4 0.6 copy-done.5
  52.9 2.1 %memory_part.1 = (f32[2,2,64,128]{3,2,1,0:T(8,128)}, f32[2,2,64,128]{3,2,1,0:T(8,128)}, f32[2,2,64,128]{3,2,1,0:T(8,128)}, f32[2,2,64,128]{3,2,1,0:T(8,128)}) custom-call(s32[1]{0:T(128)} %bitcast.hidx, f32[128,128]{1,0:T(8,128)} %get-tuple-element.62.part0, f32[128,128]{1,0:T(8,128)} %copy-done.5, bf16[64,1024]{1,0:T(8,128)(2,1)} %bitcast.55, ...), custom_call_target="tpu_custom_call" | custom-call | tf_op jit(solution)/shard_map/memory_part/pallas_call | solution.py:256
  55.0 1.6 %collective-permute-start.9 = (f32[2,2,64,128]{3,2,1,0:T(8,128)}, f32[2,2,64,128]{3,2,1,0:T(8,128)S(1)}, u32[]{:S(2)}, u32[]{:S(2)}) collective-permute-start(f32[2,2,64,128]{3,2,1,0:T(8,128)} %get-tuple-element.72), channel_id=1, source_target_pairs={{0,1},{1,0},{2,3},{3,2},{4,5},{5,4},{6,7},{7,6},{8,9},{9,8},{10,11... | collective-permute-start | bytes 393224 | tf_op jit(solution)/shard_map/ppermute | solution.py:293
  56.6 2.2 %collective-permute-start.10 = (f32[2,2,64,128]{3,2,1,0:T(8,128)}, f32[2,2,64,128]{3,2,1,0:T(8,128)S(1)}, u32[]{:S(2)}, u32[]{:S(2)}) collective-permute-start(f32[2,2,64,128]{3,2,1,0:T(8,128)} %get-tuple-element.73), channel_id=1, source_target_pairs={{0,3},{1,2},{2,1},{3,0},{4,7},{5,6},{6,5},{7,4},{8,11},{9,10},{10,... | collective-permute-start | bytes 393224 | tf_op jit(solution)/shard_map/ppermute | solution.py:293
  58.8 2.0 %collective-permute-start.11 = (f32[2,56,128]{2,1,0:T(8,128)S(1)}, f32[2,56,128]{2,1,0:T(8,128)S(1)}, u32[]{:S(2)}, u32[]{:S(2)}) collective-permute-start(f32[2,56,128]{2,1,0:T(8,128)S(1)} %fusion.14), channel_id=1, source_target_pairs={{0,48},{8,56},{16,32},{24,40},{32,16},{40,24},{48,0},{56,8},{64,11... | collective-permute-start | bytes 172040 | tf_op jit(solution)/shard_map/ppermute | solution.py:293
  60.8 0.8 %collective-permute-start.12 = (f32[2,48,128]{2,1,0:T(8,128)S(1)}, f32[2,48,128]{2,1,0:T(8,128)S(1)}, u32[]{:S(2)}, u32[]{:S(2)}) collective-permute-start(f32[2,48,128]{2,1,0:T(8,128)S(1)} %fusion.20), channel_id=1, source_target_pairs={{0,16},{8,24},{16,0},{24,8},{32,48},{40,56},{48,32},{56,40},{64,80... | collective-permute-start | bytes 147464 | tf_op jit(solution)/shard_map/ppermute | solution.py:293
  61.6 3.3 %collective-permute-done.12 = f32[2,48,128]{2,1,0:T(8,128)S(1)} collective-permute-done((f32[2,48,128]{2,1,0:T(8,128)S(1)}, f32[2,48,128]{2,1,0:T(8,128)S(1)}, u32[]{:S(2)}, u32[]{:S(2)}) %collective-permute-start.12) | collective-permute-done | bytes 49184 | tf_op jit(solution)/shard_map/ppermute | solution.py:293
  64.9 0.0 collective-permute-done.11
  64.9 0.0 collective-permute-done.9
  64.9 0.0 collective-permute-done.10
  65.0 0.6 fusion.17
  65.6 0.9 %add_bitcast_fusion.1 = f32[2,64,128]{2,1,0:T(8,128)S(1)} fusion(f32[2,2,64,128]{3,2,1,0:T(8,128)S(1)} %collective-permute-done.9, f32[2,2,64,128]{3,2,1,0:T(8,128)} %get-tuple-element.67), kind=kLoop, calls=%fused_computation.30 | loop fusion | flops 16384 | bytes 196608 | tf_op jit(solution)/shard_map/add | solution.py:338
  66.4 0.9 %add_bitcast_fusion = f32[2,64,128]{2,1,0:T(8,128)S(1)} fusion(f32[2,2,64,128]{3,2,1,0:T(8,128)S(1)} %collective-permute-done.10, f32[2,2,64,128]{3,2,1,0:T(8,128)} %get-tuple-element.77), kind=kLoop, calls=%fused_computation.29 | loop fusion | flops 16384 | bytes 196608 | tf_op jit(solution)/shard_map/add | solution.py:338
  67.3 1.1 %collective-permute-start.13 = (f32[2,64,128]{2,1,0:T(8,128)S(1)}, f32[2,64,128]{2,1,0:T(8,128)S(1)}, u32[]{:S(2)}, u32[]{:S(2)}) collective-permute-start(f32[2,64,128]{2,1,0:T(8,128)S(1)} %add_bitcast_fusion.1), channel_id=1, source_target_pairs={{0,3},{1,2},{2,1},{3,0},{4,7},{5,6},{6,5},{7,4},{8,11},{9,10},{10,... | collective-permute-start | bytes 196616 | tf_op jit(solution)/shard_map/ppermute | solution.py:293
  68.4 0.0 collective-permute-start.14
  68.4 3.5 %collective-permute-start.15 = (f32[104,128]{1,0:T(8,128)S(1)}, f32[104,128]{1,0:T(8,128)S(1)}, u32[]{:S(2)}, u32[]{:S(2)}) collective-permute-start(f32[104,128]{1,0:T(8,128)S(1)} %get-tuple-element.84), channel_id=1, source_target_pairs={{0,64},{8,72},{16,80},{24,88},{32,96},{40,104},{48,112},{56,120},{... | collective-permute-start | bytes 159752 | tf_op jit(solution)/shard_map/ppermute | solution.py:293
  72.0 2.4 %collective-permute-done.15.part1 = f32[104,128]{1,0:T(8,128)S(1)} collective-permute-done((f32[104,128]{1,0:T(8,128)S(1)}, f32[104,128]{1,0:T(8,128)S(1)}, u32[]{:S(2)}, u32[]{:S(2)}) %collective-permute-start.15) | collective-permute-done | bytes 53280 | tf_op jit(solution)/shard_map/ppermute | solution.py:293
  74.3 0.9 %bitcast_add_fusion = (f32[2,64,128]{2,1,0:T(8,128)S(1)}, f32[2,64,128]{2,1,0:T(8,128)S(1)}) fusion(f32[2,64,128]{2,1,0:T(8,128)S(1)} %collective-permute-done.14, f32[2,2,64,128]{3,2,1,0:T(8,128)S(1)} %collective-permute-done.10, f32[2,2,64,128]{3,2,1,0:T(8,128)} %get-tuple-element.77, f32[2,64,128]{2,1,0:T(8,128)S(1)} %collective-permute-done.13, ...), kind=kLoop, calls=%fused_computation.26 | loop fusion | flops 65536 | bytes 524288 | tf_op jit(solution)/shard_map/add | solution.py:349
  75.3 0.8 %collective-permute-start.16 = (f32[128,128]{1,0:T(8,128)S(1)}, f32[128,128]{1,0:T(8,128)S(1)}, u32[]{:S(2)}, u32[]{:S(2)}) collective-permute-start(f32[128,128]{1,0:T(8,128)S(1)} %get-tuple-element.93), channel_id=1, source_target_pairs={{0,4},{1,5},{2,6},{3,7},{4,0},{5,1},{6,2},{7,3},{8,12},{9,13},{10,... | collective-permute-start | bytes 196616 | tf_op jit(solution)/shard_map/ppermute | solution.py:293
  76.1 1.6 %weight_parts.1 = (f32[32,64]{1,0:T(8,128)}, f32[64,64]{1,0:T(8,128)}, f32[64,64]{1,0:T(8,128)}, f32[32,64]{1,0:T(8,128)}, f32[8,128]{1,0:T(8,128)}) custom-call(f32[104,128]{1,0:T(8,128)} %get-tuple-element.81.part0, f32[104,128]{1,0:T(8,128)} %copy-done.6), custom_call_target="tpu_custom_call" | custom-call | tf_op jit(solution)/shard_map/weight_parts/pallas_call | solution.py:282
  77.7 0.7 slice_bitcast_fusion
  78.4 1.2 %collective-permute-done.16 = f32[128,128]{1,0:T(8,128)S(1)} collective-permute-done((f32[128,128]{1,0:T(8,128)S(1)}, f32[128,128]{1,0:T(8,128)S(1)}, u32[]{:S(2)}, u32[]{:S(2)}) %collective-permute-start.16) | collective-permute-done | bytes 65568 | tf_op jit(solution)/shard_map/ppermute | solution.py:293
  79.6 0.6 add_divide_fusion
  (25 shorter events, 0.2 us)
Async XLA Ops:
  0.6 0.9 %copy-start = (bf16[1024,64]{0,1:T(8,128)(2,1)S(1)}, bf16[1024,64]{0,1:T(8,128)(2,1)}, u32[]{:S(2)}) copy-start(bf16[1024,64]{0,1:T(8,128)(2,1)} %param.11) | copy-start | bytes 393220
  1.5 0.9 %copy-start.1 = (bf16[1024,64]{0,1:T(8,128)(2,1)S(1)}, bf16[1024,64]{0,1:T(8,128)(2,1)}, u32[]{:S(2)}) copy-start(bf16[1024,64]{0,1:T(8,128)(2,1)} %param.12) | copy-start | bytes 393220
  2.5 0.8 %copy-start.2 = (bf16[512,64]{0,1:T(8,128)(2,1)S(1)}, bf16[512,64]{0,1:T(8,128)(2,1)}, u32[]{:S(2)}) copy-start(bf16[512,64]{0,1:T(8,128)(2,1)} %param.10) | copy-start | bytes 196612
  3.3 0.8 %copy-start.3 = (bf16[64,512]{1,0:T(8,128)(2,1)S(1)}, bf16[64,512]{1,0:T(8,128)(2,1)}, u32[]{:S(2)}) copy-start(bf16[64,512]{1,0:T(8,128)(2,1)} %wo_hbm.1) | copy-start | bytes 196612
  4.1 0.7 copy-start.4
  20.5 2.0 %collective-permute-start = (f32[8,128,128]{2,1,0:T(8,128)S(1)}, f32[8,128,128]{2,1,0:T(8,128)S(1)}, u32[]{:S(2)}, u32[]{:S(2)}) collective-permute-start(f32[8,128,128]{2,1,0:T(8,128)S(1)} %get-tuple-element.51), channel_id=1, source_target_pairs={{0,8},{8,0},{16,24},{24,16},{32,40},{40,32},{48,56},{56,48},{64,72... | collective-permute-start | bytes 1572872 | tf_op jit(solution)/shard_map/ppermute | solution.py:293
  22.6 11.9 %collective-permute-start.3 = (f32[8,104,128]{2,1,0:T(8,128)S(1)}, f32[8,104,128]{2,1,0:T(8,128)S(1)}, u32[]{:S(2)}, u32[]{:S(2)}) collective-permute-start(f32[8,104,128]{2,1,0:T(8,128)S(1)} %get-tuple-element.55), channel_id=1, source_target_pairs={{0,8},{8,0},{16,24},{24,16},{32,40},{40,32},{48,56},{56,48},{64,72... | collective-permute-start | bytes 1277960 | tf_op jit(solution)/shard_map/ppermute | solution.py:293
  22.8 8.0 %collective-permute-start.1 = (f32[2,2,64,128]{3,2,1,0:T(8,128)S(1)}, f32[2,2,64,128]{3,2,1,0:T(8,128)S(1)}, u32[]{:S(2)}, u32[]{:S(2)}) collective-permute-start(f32[2,2,64,128]{3,2,1,0:T(8,128)S(1)} %slice.149), channel_id=1, source_target_pairs={{0,16},{8,24},{16,0},{24,8},{32,48},{40,56},{48,32},{56,40},{64,80... | collective-permute-start | bytes 393224 | tf_op jit(solution)/shard_map/ppermute | solution.py:293
  26.8 7.7 %collective-permute-start.2 = (f32[2,2,64,128]{3,2,1,0:T(8,128)S(1)}, f32[2,2,64,128]{3,2,1,0:T(8,128)S(1)}, u32[]{:S(2)}, u32[]{:S(2)}) collective-permute-start(f32[2,2,64,128]{3,2,1,0:T(8,128)S(1)} %pad_maximum_fusion), channel_id=1, source_target_pairs={{0,48},{8,56},{16,32},{24,40},{32,16},{40,24},{48,0},{56,8},{64,11... | collective-permute-start | bytes 393224 | tf_op jit(solution)/shard_map/ppermute | solution.py:293
  34.6 5.6 %collective-permute-start.4 = (f32[2,64,128]{2,1,0:T(8,128)S(1)}, f32[2,64,128]{2,1,0:T(8,128)S(1)}, u32[]{:S(2)}, u32[]{:S(2)}) collective-permute-start(f32[2,64,128]{2,1,0:T(8,128)S(1)} %get-tuple-element.58), channel_id=1, source_target_pairs={{0,48},{8,56},{16,32},{24,40},{32,16},{40,24},{48,0},{56,8},{64,11... | collective-permute-start | bytes 196616 | tf_op jit(solution)/shard_map/ppermute | solution.py:293
  37.6 4.3 %collective-permute-start.5 = (f32[2,64,128]{2,1,0:T(8,128)S(1)}, f32[2,64,128]{2,1,0:T(8,128)S(1)}, u32[]{:S(2)}, u32[]{:S(2)}) collective-permute-start(f32[2,64,128]{2,1,0:T(8,128)S(1)} %get-tuple-element.59), channel_id=1, source_target_pairs={{0,16},{8,24},{16,0},{24,8},{32,48},{40,56},{48,32},{56,40},{64,80... | collective-permute-start | bytes 196616 | tf_op jit(solution)/shard_map/ppermute | solution.py:293
  42.6 9.8 %collective-permute-start.7 = (f32[2,2,56,128]{3,2,1,0:T(8,128)S(1)}, f32[2,2,56,128]{3,2,1,0:T(8,128)S(1)}, u32[]{:S(2)}, u32[]{:S(2)}) collective-permute-start(f32[2,2,56,128]{3,2,1,0:T(8,128)S(1)} %slice.157), channel_id=1, source_target_pairs={{0,16},{8,24},{16,0},{24,8},{32,48},{40,56},{48,32},{56,40},{64,80... | collective-permute-start | bytes 344072 | tf_op jit(solution)/shard_map/ppermute | solution.py:293
  42.6 9.8 %collective-permute-start.8 = (f32[2,2,48,128]{3,2,1,0:T(8,128)S(1)}, f32[2,2,48,128]{3,2,1,0:T(8,128)S(1)}, u32[]{:S(2)}, u32[]{:S(2)}) collective-permute-start(f32[2,2,48,128]{3,2,1,0:T(8,128)S(1)} %pad_maximum_fusion.1), channel_id=1, source_target_pairs={{0,48},{8,56},{16,32},{24,40},{32,16},{40,24},{48,0},{56,8},{64,11... | collective-permute-start | bytes 294920 | tf_op jit(solution)/shard_map/ppermute | solution.py:293
  43.8 8.5 %collective-permute-start.6 = (f32[128,128]{1,0:T(8,128)S(1)}, f32[128,128]{1,0:T(8,128)S(1)}, u32[]{:S(2)}, u32[]{:S(2)}) collective-permute-start(f32[128,128]{1,0:T(8,128)S(1)} %get-tuple-element.63), channel_id=1, source_target_pairs={{0,64},{8,72},{16,80},{24,88},{32,96},{40,104},{48,112},{56,120},{... | collective-permute-start | bytes 196616 | tf_op jit(solution)/shard_map/ppermute | solution.py:293
  52.3 0.6 copy-start.5
  55.0 9.9 %collective-permute-start.9 = (f32[2,2,64,128]{3,2,1,0:T(8,128)}, f32[2,2,64,128]{3,2,1,0:T(8,128)S(1)}, u32[]{:S(2)}, u32[]{:S(2)}) collective-permute-start(f32[2,2,64,128]{3,2,1,0:T(8,128)} %get-tuple-element.72), channel_id=1, source_target_pairs={{0,1},{1,0},{2,3},{3,2},{4,5},{5,4},{6,7},{7,6},{8,9},{9,8},{10,11... | collective-permute-start | bytes 393224 | tf_op jit(solution)/shard_map/ppermute | solution.py:293
  56.6 8.3 %collective-permute-start.10 = (f32[2,2,64,128]{3,2,1,0:T(8,128)}, f32[2,2,64,128]{3,2,1,0:T(8,128)S(1)}, u32[]{:S(2)}, u32[]{:S(2)}) collective-permute-start(f32[2,2,64,128]{3,2,1,0:T(8,128)} %get-tuple-element.73), channel_id=1, source_target_pairs={{0,3},{1,2},{2,1},{3,0},{4,7},{5,6},{6,5},{7,4},{8,11},{9,10},{10,... | collective-permute-start | bytes 393224 | tf_op jit(solution)/shard_map/ppermute | solution.py:293
  58.8 6.1 %collective-permute-start.11 = (f32[2,56,128]{2,1,0:T(8,128)S(1)}, f32[2,56,128]{2,1,0:T(8,128)S(1)}, u32[]{:S(2)}, u32[]{:S(2)}) collective-permute-start(f32[2,56,128]{2,1,0:T(8,128)S(1)} %fusion.14), channel_id=1, source_target_pairs={{0,48},{8,56},{16,32},{24,40},{32,16},{40,24},{48,0},{56,8},{64,11... | collective-permute-start | bytes 172040 | tf_op jit(solution)/shard_map/ppermute | solution.py:293
  60.8 4.1 %collective-permute-start.12 = (f32[2,48,128]{2,1,0:T(8,128)S(1)}, f32[2,48,128]{2,1,0:T(8,128)S(1)}, u32[]{:S(2)}, u32[]{:S(2)}) collective-permute-start(f32[2,48,128]{2,1,0:T(8,128)S(1)} %fusion.20), channel_id=1, source_target_pairs={{0,16},{8,24},{16,0},{24,8},{32,48},{40,56},{48,32},{56,40},{64,80... | collective-permute-start | bytes 147464 | tf_op jit(solution)/shard_map/ppermute | solution.py:293
  67.3 7.0 %collective-permute-start.13 = (f32[2,64,128]{2,1,0:T(8,128)S(1)}, f32[2,64,128]{2,1,0:T(8,128)S(1)}, u32[]{:S(2)}, u32[]{:S(2)}) collective-permute-start(f32[2,64,128]{2,1,0:T(8,128)S(1)} %add_bitcast_fusion.1), channel_id=1, source_target_pairs={{0,3},{1,2},{2,1},{3,0},{4,7},{5,6},{6,5},{7,4},{8,11},{9,10},{10,... | collective-permute-start | bytes 196616 | tf_op jit(solution)/shard_map/ppermute | solution.py:293
  68.4 5.9 %collective-permute-start.14 = (f32[2,64,128]{2,1,0:T(8,128)S(1)}, f32[2,64,128]{2,1,0:T(8,128)S(1)}, u32[]{:S(2)}, u32[]{:S(2)}) collective-permute-start(f32[2,64,128]{2,1,0:T(8,128)S(1)} %add_bitcast_fusion), channel_id=1, source_target_pairs={{0,1},{1,0},{2,3},{3,2},{4,5},{5,4},{6,7},{7,6},{8,9},{9,8},{10,11... | collective-permute-start | bytes 196616 | tf_op jit(solution)/shard_map/ppermute | solution.py:293
  68.4 5.9 %collective-permute-start.15 = (f32[104,128]{1,0:T(8,128)S(1)}, f32[104,128]{1,0:T(8,128)S(1)}, u32[]{:S(2)}, u32[]{:S(2)}) collective-permute-start(f32[104,128]{1,0:T(8,128)S(1)} %get-tuple-element.84), channel_id=1, source_target_pairs={{0,64},{8,72},{16,80},{24,88},{32,96},{40,104},{48,112},{56,120},{... | collective-permute-start | bytes 159752 | tf_op jit(solution)/shard_map/ppermute | solution.py:293
  74.3 1.8 %copy-start.6 = (f32[104,128]{1,0:T(8,128)}, f32[104,128]{1,0:T(8,128)S(1)}, u32[]{:S(2)}) copy-start(f32[104,128]{1,0:T(8,128)S(1)} %collective-permute-done.15.part1) | copy-start | bytes 159748
  75.3 4.3 %collective-permute-start.16 = (f32[128,128]{1,0:T(8,128)S(1)}, f32[128,128]{1,0:T(8,128)S(1)}, u32[]{:S(2)}, u32[]{:S(2)}) collective-permute-start(f32[128,128]{1,0:T(8,128)S(1)} %get-tuple-element.93), channel_id=1, source_target_pairs={{0,4},{1,5},{2,6},{3,7},{4,0},{5,1},{6,2},{7,3},{8,12},{9,13},{10,... | collective-permute-start | bytes 196616 | tf_op jit(solution)/shard_map/ppermute | solution.py:293

commit v3 on v2

--- a/solution.py
+++ b/solution.py
@@ -31,9 +31,9 @@
 
 
 def main_kernel(
-    sidx, masked, q_hbm, g_hbm, mem_hbm, wq_hbm, wk_hbm, wv_hbm, wo_hbm,
+    sidx, masked_hbm, q_hbm, g_hbm, mem_hbm, wq_hbm, wk_hbm, wv_hbm, wo_hbm,
     keep_a, send_a, keep_b, send_b,
-    q_in, g_in, mem, qc, gc, kv, wkv, wq2, wo2, pos, off_v, off_s,
+    masked, q_in, g_in, mem, qc, gc, kv, wkv, wq2, wo2, pos, off_v, off_s,
     dkv, wqo, wkv_out, wqo_out,
     mem_sem, row_sem, w_sem, off_sem,
 ):
@@ -66,12 +66,15 @@
         ]
         for i in range(ROW_PARTS)
     ]
+    mask_copy = pltpu.make_async_copy(masked_hbm, masked, off_sem)
+    mask_copy.start()
     for c in w_copies + mem_copies:
         c.start()
     for pair in row_copies:
         for c in pair:
             c.start()
 
+    mask_copy.wait()
     ones = masked[...].astype(f32)
     mb = ones.astype(bf16)
     r128 = lax.broadcasted_iota(jnp.int32, (128, 128), 0)
@@ -184,30 +187,42 @@
                 chunk = piece if chunk is None else jnp.where(lane32 >= 32 * k, piece, chunk)
             wqo_out[4 * t + u] = chunk
     count = jnp.zeros((8, 128), f32) + total.astype(f32)
+    core = me & 1
     for p in range(16):
-        rc, rx, rz = p // 8, (p // 2) % 4, p % 2
-        s = me ^ (rz * 8 + rx * 2 + rc)
+        i, rc = p % 8, p // 8
+        z, x = i // 4, i % 4
         a = (keep_a, send_a)[rc]
         b = (keep_b, send_b)[rc]
-        i = p % 8
+        s = z * 8 + x * 2 + (core ^ rc)
         a[i] = dkv[:, pl.ds(pl.multiple_of(s * 128, 128), 128)]
+        s = me ^ (z * 8 + x * 2 + rc)
         b[i, 0:64] = wkv_out[s]
         b[i, 64:96] = wqo_out[s]
         b[i, 96:104] = count
 
 
+def in_hbm(x):
+    return pltpu.with_memory_space_constraint(x, pltpu.HBM)
+
+
+def in_vmem(x):
+    return pltpu.with_memory_space_constraint(x, pltpu.VMEM)
+
+
 def run_main(sidx, masked, queries, grads, memory, w_query, w_key, w_value, w_out):
     any_ = pl.BlockSpec(memory_space=pl.ANY)
     vm = pl.BlockSpec(memory_space=pltpu.VMEM)
-    a = jax.ShapeDtypeStruct((8, 128, 128), f32)
-    b = jax.ShapeDtypeStruct((8, 104, 128), f32)
+    a = pltpu.VMEM((8, 128, 128), f32)
+    b = pltpu.VMEM((8, 104, 128), f32)
+    arrays = [in_hbm(x) for x in (queries, grads, memory, w_query, w_key, w_value, w_out)]
     pad = ROWS + LARGE + TB
     return pl.pallas_call(
         main_kernel,
         out_shape=(a, a, b, b),
-        in_specs=[pl.BlockSpec(memory_space=pltpu.SMEM), vm] + [any_] * 7,
+        in_specs=[pl.BlockSpec(memory_space=pltpu.SMEM)] + [any_] * 8,
         out_specs=(vm,) * 4,
         scratch_shapes=[
+            pltpu.VMEM((32, 128), jnp.int32),
             pltpu.VMEM((ROWS, E), bf16),
             pltpu.VMEM((ROWS, E), bf16),
             pltpu.VMEM((LAT, C), bf16),
@@ -232,60 +247,58 @@
         compiler_params=pltpu.CompilerParams(vmem_limit_bytes=48 * 1024 * 1024),
         cost_estimate=pl.CostEstimate(flops=10**10, bytes_accessed=14 * 2**20, transcendentals=10**7),
         name="masked_rows",
-    )(sidx, masked, queries, grads, memory, w_query, w_key, w_value, w_out)
-
-
-def head_kernel(hidx, part0, part1, wk, wv, keep_al, send_al, keep_be, send_be):
-    me = hidx[0]
-    dt = (part0[...] + part1[...]).T.astype(bf16)
-    for ry in range(4):
-        for rz in range(2):
-            c = me ^ (rz * 4 + ry)
-            cols = pl.ds(pl.multiple_of(c * 128, 128), 128)
-            w = jnp.concatenate([wk[:, cols], wv[:, cols]], axis=0)
-            out = _dot(dt, w, NN)
-            al = (keep_al, 0) if ry == 0 else (keep_al, 1) if ry == 3 else (send_al, ry - 1)
-            be = (keep_be, ry) if ry < 2 else (send_be, 3 - ry)
-            al[0][al[1], rz] = out[:64]
-            be[0][be[1], rz] = out[64:]
-
-
-def run_head(hidx, part0, part1, wk_t, wv_t):
+    )(sidx, in_hbm(masked), *arrays)
+
+
+def head_kernel(parts, wk, wv, out):
+    d = parts[0]
+    for k in range(1, 8):
+        d = d + parts[k]
+    dt = d.T.astype(bf16)
+    for c in range(8):
+        cols = slice(128 * c, 128 * (c + 1))
+        w = jnp.concatenate([wk[:, cols], wv[:, cols]], axis=0)
+        out[c] = _dot(dt, w, NN)
+
+
+def run_head(parts, wk_t, wv_t):
     vm = pl.BlockSpec(memory_space=pltpu.VMEM)
-    o = jax.ShapeDtypeStruct((2, 2, 64, 128), f32)
     return pl.pallas_call(
         head_kernel,
-        out_shape=(o,) * 4,
-        in_specs=[pl.BlockSpec(memory_space=pltpu.SMEM)] + [vm] * 4,
-        out_specs=(vm,) * 4,
+        out_shape=pltpu.VMEM((8, 128, 128), f32),
+        in_specs=[vm] * 3,
+        out_specs=vm,
         name="memory_part",
-    )(hidx, part0, part1, wk_t, wv_t)
-
-
-def weights_kernel(part0, part1, gwq, gwk, gwv, gwo_t, total):
-    b = part0[...] + part1[...]
-    count = b[96:104, :]
-    total[...] = count
-    b = b / count[0:1, :]
+    )(in_vmem(parts), in_vmem(wk_t), in_vmem(wv_t))
+
+
+def last_kernel(mine, got, parts, gwq, gwk, gwv, gwo_t, gmem):
+    b = mine[...] + got[...]
+    scale = 1.0 / b[96:97, :]
+    b = b * scale
     kv_t = b[0:64].T
     gwk[...] = kv_t[:64]
     gwv[...] = kv_t[64:]
     qo_t = b[64:96].T
     gwq[...] = jnp.concatenate([qo_t[0:32], qo_t[64:96]], axis=1)
     gwo_t[...] = jnp.concatenate([qo_t[32:64], qo_t[96:128]], axis=1)
-
-
-def run_weights(part0, part1):
+    m = parts[0]
+    for k in range(1, 8):
+        m = m + parts[k]
+    gmem[...] = m * scale
+
+
+def run_last(mine, got, parts):
     vm = pl.BlockSpec(memory_space=pltpu.VMEM)
     small = jax.ShapeDtypeStruct((32, 64), f32)
     square = jax.ShapeDtypeStruct((64, 64), f32)
     return pl.pallas_call(
-        weights_kernel,
-        out_shape=(small, square, square, small, jax.ShapeDtypeStruct((8, 128), f32)),
-        in_specs=[vm] * 2,
+        last_kernel,
+        out_shape=(small, square, square, small, jax.ShapeDtypeStruct((128, 128), f32)),
+        in_specs=[vm] * 3,
         out_specs=(vm,) * 5,
-        name="weight_parts",
-    )(part0, part1)
+        name="gradients",
+    )(in_vmem(mine), in_vmem(got), in_vmem(parts))
 
 
 def swap(x, axis, bits):
@@ -298,60 +311,26 @@
 
 def shards(queries, memory, w_query, w_key, w_value, w_out, grad_out, masked):
     seq = lax.axis_index("seq").astype(jnp.int32).reshape(1)
-    head = lax.axis_index("head").astype(jnp.int32).reshape(1)
     wk_t, wv_t = w_key.T, w_value.T
     keep_a, send_a, keep_b, send_b = run_main(
         seq, masked.reshape(32, 128), queries, grad_out, memory, w_query.T, wk_t, wv_t, w_out
     )
     got_a = swap(send_a, "seq", 1)
-    sum_a = hold(keep_a + got_a).reshape(4, 2, 128, 128)
-    al_send, be_send = sum_a[1:3, :, :64], jnp.stack([sum_a[3, :, 64:], sum_a[2, :, 64:]])
-    al_send, be_send, send_b = hold((al_send, be_send, send_b))
-    al_in = swap(al_send, "seq", 2)
-    be_in = swap(be_send, "seq", 6)
     got_b = swap(send_b, "seq", 1)
-    al_in, be_in, got_b = hold((al_in, be_in, got_b))
-
-    al_send, be_send = hold((sum_a[3, :, :64] + al_in[1], sum_a[1, :, 64:] + be_in[1]))
-    al_in2 = swap(al_send, "seq", 6)
-    be_in2 = swap(be_send, "seq", 2)
-    sum_b = hold(keep_b + got_b).reshape(4, 2, 104, 128)
-    bl_send, bh_send = sum_b[1:3, :, :56], jnp.stack([sum_b[3, :, 56:], sum_b[2, :, 56:]])
-    al = sum_a[0, :, :64] + al_in[0] + al_in2
-    be = sum_a[0, :, 64:] + be_in[0] + be_in2
-    sums = jnp.concatenate([al, be], axis=1)
-    mine, send, bl_send, bh_send = hold((sums[0], sums[1], bl_send, bh_send))
+    groups = [[z * 8 + x * 2 + core for z in range(2) for x in range(4)] for core in range(2)]
+    sum_a, sum_b = hold((keep_a + got_a, keep_b + got_b))
+    sum_b = sum_b.reshape(2, 4, 104, 128)
+    sends = hold((sum_b[:, 1], sum_b[:, 3], sum_b[:, 2]))
+    ins = [swap(x, "seq", bits) for x, bits in zip(sends, (2, 6, 4))]
+    parts = lax.all_to_all(sum_a, "seq", 0, 0, axis_index_groups=groups)
+    parts, ins = hold((parts, ins))
+    part = run_head(parts, wk_t, wv_t)
+
+    sum_b = sum_b[:, 0] + ins[0] + ins[1] + ins[2]
+    part, mine, send = hold((part, sum_b[0], sum_b[1]))
     got = swap(send, "seq", 8)
-    bl_in = swap(bl_send, "seq", 2)
-    bh_in = swap(bh_send, "seq", 6)
-    got, bl_in, bh_in = hold((got, bl_in, bh_in))
-
-    keep_al, send_al, keep_be, send_be = run_head(head, mine, got, wk_t, wv_t)
-    bl_send, bh_send = sum_b[3, :, :56] + bl_in[1], sum_b[1, :, 56:] + bh_in[1]
-    send_al, send_be, bl_send, bh_send = hold((send_al, send_be, bl_send, bh_send))
-    ml_in = swap(send_al, "head", 1)
-    mh_in = swap(send_be, "head", 3)
-    bl_in2 = swap(bl_send, "seq", 6)
-    bh_in2 = swap(bh_send, "seq", 2)
-    ml_in, mh_in, bl_in2, bh_in2 = hold((ml_in, mh_in, bl_in2, bh_in2))
-
-    ml_send, mh_send = keep_al[1] + ml_in[1], keep_be[1] + mh_in[1]
-    bl = sum_b[0, :, :56] + bl_in[0] + bl_in2
-    bh = sum_b[0, :, 56:] + bh_in[0] + bh_in2
-    sums = jnp.concatenate([bl, bh], axis=1)
-    ml_send, mh_send, mine_b, send_b = hold((ml_send, mh_send, sums[0], sums[1]))
-    ml_in2 = swap(ml_send, "head", 3)
-    mh_in2 = swap(mh_send, "head", 1)
-    got_b = swap(send_b, "seq", 8)
-    ml_in2, mh_in2, got_b = hold((ml_in2, mh_in2, got_b))
-
-    ml = keep_al[0] + ml_in[0] + ml_in2
-    mh = keep_be[0] + mh_in[0] + mh_in2
-    mem = jnp.concatenate([ml, mh], axis=1)
-    mine, send = hold((mem[0], mem[1]))
-    got = swap(send, "head", 4)
-    grad_wq, grad_wk, grad_wv, grad_wo_t, total = run_weights(mine_b, got_b)
-    grad_memory = (mine + got) / total[0:1, :]
+    parts = lax.all_to_all(part, "head", 0, 0)
+    grad_wq, grad_wk, grad_wv, grad_wo_t, grad_memory = run_last(mine, got, parts)
     return (grad_wq, grad_wk, grad_wv, grad_wo_t.T, grad_memory)
 
 

time: 81.5 us -> 67.3 us (0.83)
  local copies, waits for them, and re-layouts: 5.49 us -> 0.04 us
  other arithmetic: 4.75 us -> 0.92 us
  waiting for transfers between devices: 19.2 us -> 17.3 us
  starting transfers between devices: 30.6 us -> 28.8 us
    ppermute x17 -> x6, starting transfers between devices: 30.6 us -> 8.93 us  [swap(): return lax.ppermute(x, axis, [(i, i ^ bits) for i in range(n)])]
    all_to_all x0 -> x2, starting transfers between devices: none -> 19.8 us  [the longest x1 14.9 us: shards(): parts = lax.all_to_all(sum_a, 'seq', 0, 0, axis_index_groups=groups)]
    unnamed x14 -> x4, local copies, waits for them, and re-layouts: 4.78 us -> 0.01 us
    ppermute x17 -> x6, waiting for transfers between devices: 19.2 us -> 17.2 us  [swap(): return lax.ppermute(x, axis, [(i, i ^ bits) for i in range(n)])]
    add x11 -> x3, other arithmetic: 2.81 us -> 0.92 us  [the longest x2 0.89 us: shards(): sum_a, sum_b = hold((keep_a + got_a, keep_b + got_b))]
    pallas_call x2, Pallas kernels: 3.74 us -> 1.91 us  [the longest x1 1.09 us: run_head(): pl.pallas_call(head_kernel, out_shape=pltpu.VMEM((8, 128, 128), f32), in_...]
    squeeze x3 -> x0, other arithmetic: 1.28 us -> none  [the longest x1 0.64 us: shards(): mine, send, bl_send, bh_send = hold((sums[0], sums[1], bl_send, bh_send))]
    pallas_call x1, Pallas kernels: 15.6 us -> 16.8 us  [run_main(): pl.pallas_call(main_kernel, out_shape=(a, a, b, b), in_specs=[pl.BlockSpe...]
  transfers between devices with their start and end apart: 17 -> 8, of which waited for: 9 -> 6; matrix products, arithmetic and copies ran while one was open for 1% -> 0% of each run, Pallas kernels for 2% -> 0%
where the time goes in v3:
time: 67.3 us; the launch traced here: 66.5 us
  starting transfers between devices  28.8 us (43%)
  Pallas kernels  18.7 us (28%)
  waiting for transfers between devices  17.3 us (26%)
  other arithmetic  0.92 us (1%)
  between operations  0.7 us (1%)
    ppermute x6, waiting for transfers between devices, swap(): return lax.ppermute(x, axis, [(i, i ^ bits) for i in range(n)])  17.2 us
    pallas_call x1, Pallas kernels, run_main(): pl.pallas_call(main_kernel, out_shape=(a, a, b, b), in_specs=[pl.BlockSpe...  16.8 us
    all_to_all x1, starting transfers between devices, shards(): parts = lax.all_to_all(sum_a, 'seq', 0, 0, axis_index_groups=groups)  14.9 us
    ppermute x6, starting transfers between devices, swap(): return lax.ppermute(x, axis, [(i, i ^ bits) for i in range(n)])  8.93 us
    all_to_all x1, starting transfers between devices, shards(): parts = lax.all_to_all(part, 'head', 0, 0)  4.94 us
  transfers between devices with their start and end apart: 8, of which 6 were waited for; matrix products, arithmetic and copies ran while one was open for 0% of the time, Pallas kernels for 0%

profile of v3, /device:TPU:0, one launch (start us, length us, event | category | flops | bytes accessed | tf_op | source)
XLA Modules:
  0.0 66.5 jit_solution(11462566659867949779)
XLA Ops:
  0.6 16.8 %masked_rows.1 = (f32[8,128,128]{2,1,0:T(8,128)S(1)}, f32[8,128,128]{2,1,0:T(8,128)S(1)}, f32[8,104,128]{2,1,0:T(8,128)S(1)}, f32[8,104,128]{2,1,0:T(8,128)S(1)}) custom-call(s32[1]{0:T(128)} %bitcast.sidx, s32[32,128]{1,0:T(8,128)} %bitcast.40, bf16[4096,512]{1,0:T(8,128)(2,1)} %q_hbm.1, bf16[4096,512]{1,0:T(8,128)(2,1)} %g_hbm.1, ...), custom_call_target="tpu_custom_call" | custom-call | flops 10000000000 | bytes 14680064 | tf_op jit(solution)/shard_map/masked_rows/pallas_call | solution.py:219
  17.5 0.0 copy-start
  17.5 0.0 copy-start.1
  17.5 0.1 collective-permute-start
  17.6 0.5 collective-permute-start.1
  18.1 2.0 %collective-permute-done.1 = f32[8,104,128]{2,1,0:T(8,128)S(1)} collective-permute-done((f32[8,104,128]{2,1,0:T(8,128)S(1)}, f32[8,104,128]{2,1,0:T(8,128)S(1)}, u32[]{:S(2)}, u32[]{:S(2)}) %collective-permute-start.1) | collective-permute-done | bytes 426016 | tf_op jit(solution)/shard_map/ppermute | solution.py:306
  20.1 0.0 collective-permute-done
  20.2 0.8 %add.15 = f32[8,128,128]{2,1,0:T(8,128)} add(f32[8,128,128]{2,1,0:T(8,128)S(1)} %get-tuple-element.26, f32[8,128,128]{2,1,0:T(8,128)S(1)} %collective-permute-done) | non-fusion elementwise | flops 131072 | bytes 1572864 | tf_op jit(solution)/shard_map/add | solution.py:321
  21.0 14.9 %all-to-all-start = ((f32[8,128,128]{2,1,0:T(8,128)}), f32[8,128,128]{2,1,0:T(8,128)S(1)}, u32[]{:S(2)}, u32[]{:S(2)}) async-start(f32[8,128,128]{2,1,0:T(8,128)} %add.15), calls=%async_computation | async-start | bytes 1048576 | tf_op jit(solution)/shard_map/all_to_all | solution.py:325
  35.9 2.1 %collective-permute-start.2 = (f32[2,104,128]{2,1,0:T(8,128)S(1)}, f32[2,104,128]{2,1,0:T(8,128)S(1)}, u32[]{:S(2)}, u32[]{:S(2)}) collective-permute-start(f32[2,104,128]{2,1,0:T(8,128)S(1)} %get-tuple-element.32), channel_id=1, source_target_pairs={{0,16},{8,24},{16,0},{24,8},{32,48},{40,56},{48,32},{56,40},{64,80... | collective-permute-start | bytes 319496 | tf_op jit(solution)/shard_map/ppermute | solution.py:306
  38.0 2.1 %collective-permute-start.3 = (f32[2,104,128]{2,1,0:T(8,128)S(1)}, f32[2,104,128]{2,1,0:T(8,128)S(1)}, u32[]{:S(2)}, u32[]{:S(2)}) collective-permute-start(f32[2,104,128]{2,1,0:T(8,128)S(1)} %get-tuple-element.33), channel_id=1, source_target_pairs={{0,48},{8,56},{16,32},{24,40},{32,16},{40,24},{48,0},{56,8},{64,11... | collective-permute-start | bytes 319496 | tf_op jit(solution)/shard_map/ppermute | solution.py:306
  40.1 0.6 collective-permute-start.4
  40.7 6.9 %collective-permute-done.2 = f32[2,104,128]{2,1,0:T(8,128)S(1)} collective-permute-done((f32[2,104,128]{2,1,0:T(8,128)S(1)}, f32[2,104,128]{2,1,0:T(8,128)S(1)}, u32[]{:S(2)}, u32[]{:S(2)}) %collective-permute-start.2) | collective-permute-done | bytes 106528 | tf_op jit(solution)/shard_map/ppermute | solution.py:306
  47.6 0.8 %collective-permute-done.3 = f32[2,104,128]{2,1,0:T(8,128)S(1)} collective-permute-done((f32[2,104,128]{2,1,0:T(8,128)S(1)}, f32[2,104,128]{2,1,0:T(8,128)S(1)}, u32[]{:S(2)}, u32[]{:S(2)}) %collective-permute-start.3) | collective-permute-done | bytes 106528 | tf_op jit(solution)/shard_map/ppermute | solution.py:306
  48.4 1.9 %collective-permute-done.4 = f32[2,104,128]{2,1,0:T(8,128)S(1)} collective-permute-done((f32[2,104,128]{2,1,0:T(8,128)S(1)}, f32[2,104,128]{2,1,0:T(8,128)S(1)}, u32[]{:S(2)}, u32[]{:S(2)}) %collective-permute-start.4) | collective-permute-done | bytes 106528 | tf_op jit(solution)/shard_map/ppermute | solution.py:306
  50.3 0.0 all-to-all-done.parts
  50.3 0.0 copy-done
  50.3 0.0 copy-done.1
  50.3 1.1 %memory_part.1 = f32[8,128,128]{2,1,0:T(8,128)} custom-call(f32[8,128,128]{2,1,0:T(8,128)S(1)} %all-to-all-done.parts, bf16[64,1024]{1,0:T(8,128)(2,1)S(1)} %bitcast.34, bf16[64,1024]{1,0:T(8,128)(2,1)S(1)} %bitcast.36), custom_call_target="tpu_custom_call" | custom-call | tf_op jit(solution)/shard_map/memory_part/pallas_call | solution.py:266
  51.4 4.9 %all-to-all-start.1 = ((f32[8,128,128]{2,1,0:T(8,128)}), f32[8,128,128]{2,1,0:T(8,128)S(1)}, u32[]{:S(2)}, u32[]{:S(2)}) async-start(f32[8,128,128]{2,1,0:T(8,128)} %memory_part.1), calls=%async_computation.1 | async-start | bytes 1048576 | tf_op jit(solution)/shard_map/all_to_all | solution.py:332
  56.4 3.6 %collective-permute-start.5 = (f32[104,128]{1,0:T(8,128)S(1)}, f32[104,128]{1,0:T(8,128)S(1)}, u32[]{:S(2)}, u32[]{:S(2)}) collective-permute-start(f32[104,128]{1,0:T(8,128)S(1)} %get-tuple-element.40), channel_id=1, source_target_pairs={{0,64},{8,72},{16,80},{24,88},{32,96},{40,104},{48,112},{56,120},{... | collective-permute-start | bytes 159752 | tf_op jit(solution)/shard_map/ppermute | solution.py:306
  59.9 5.6 %collective-permute-done.5.got = f32[104,128]{1,0:T(8,128)S(1)} collective-permute-done((f32[104,128]{1,0:T(8,128)S(1)}, f32[104,128]{1,0:T(8,128)S(1)}, u32[]{:S(2)}, u32[]{:S(2)}) %collective-permute-start.5) | collective-permute-done | bytes 53280 | tf_op jit(solution)/shard_map/ppermute | solution.py:306
  65.5 0.1 all-to-all-done.1.parts
  65.7 0.8 %gradients.1 = (f32[32,64]{1,0:T(8,128)}, f32[64,64]{1,0:T(8,128)}, f32[64,64]{1,0:T(8,128)}, f32[32,64]{1,0:T(8,128)}, f32[128,128]{1,0:T(8,128)}) custom-call(f32[104,128]{1,0:T(8,128)S(1)} %get-tuple-element.39.mine, f32[104,128]{1,0:T(8,128)S(1)} %collective-permute-done.5.got, f32[8,128,128]{2,1,0:T(8,128)S(1)} %all-to-all-done.1.parts), custom_call_target="tpu_custom_call" | custom-call | tf_op jit(solution)/shard_map/gradients/pallas_call | solution.py:295
  (4 shorter events, 0.1 us)
Async XLA Ops:
  17.5 32.8 %copy-start = (bf16[1024,64]{0,1:T(8,128)(2,1)S(1)}, bf16[1024,64]{0,1:T(8,128)(2,1)}, u32[]{:S(2)}) copy-start(bf16[1024,64]{0,1:T(8,128)(2,1)} %param.11) | copy-start | bytes 393220
  17.5 32.8 %copy-start.1 = (bf16[1024,64]{0,1:T(8,128)(2,1)S(1)}, bf16[1024,64]{0,1:T(8,128)(2,1)}, u32[]{:S(2)}) copy-start(bf16[1024,64]{0,1:T(8,128)(2,1)} %param.12) | copy-start | bytes 393220
  17.5 2.7 %collective-permute-start = (f32[8,128,128]{2,1,0:T(8,128)S(1)}, f32[8,128,128]{2,1,0:T(8,128)S(1)}, u32[]{:S(2)}, u32[]{:S(2)}) collective-permute-start(f32[8,128,128]{2,1,0:T(8,128)S(1)} %get-tuple-element.27), channel_id=1, source_target_pairs={{0,8},{8,0},{16,24},{24,16},{32,40},{40,32},{48,56},{56,48},{64,72... | collective-permute-start | bytes 1572872 | tf_op jit(solution)/shard_map/ppermute | solution.py:306
  17.6 2.5 %collective-permute-start.1 = (f32[8,104,128]{2,1,0:T(8,128)S(1)}, f32[8,104,128]{2,1,0:T(8,128)S(1)}, u32[]{:S(2)}, u32[]{:S(2)}) collective-permute-start(f32[8,104,128]{2,1,0:T(8,128)S(1)} %get-tuple-element.29), channel_id=1, source_target_pairs={{0,8},{8,0},{16,24},{24,16},{32,40},{40,32},{48,56},{56,48},{64,72... | collective-permute-start | bytes 1277960 | tf_op jit(solution)/shard_map/ppermute | solution.py:306
  21.0 29.3 %all-to-all-start = ((f32[8,128,128]{2,1,0:T(8,128)}), f32[8,128,128]{2,1,0:T(8,128)S(1)}, u32[]{:S(2)}, u32[]{:S(2)}) async-start(f32[8,128,128]{2,1,0:T(8,128)} %add.15), calls=%async_computation | async-start | bytes 1048576 | tf_op jit(solution)/shard_map/all_to_all | solution.py:325
  35.9 11.7 %collective-permute-start.2 = (f32[2,104,128]{2,1,0:T(8,128)S(1)}, f32[2,104,128]{2,1,0:T(8,128)S(1)}, u32[]{:S(2)}, u32[]{:S(2)}) collective-permute-start(f32[2,104,128]{2,1,0:T(8,128)S(1)} %get-tuple-element.32), channel_id=1, source_target_pairs={{0,16},{8,24},{16,0},{24,8},{32,48},{40,56},{48,32},{56,40},{64,80... | collective-permute-start | bytes 319496 | tf_op jit(solution)/shard_map/ppermute | solution.py:306
  38.0 10.4 %collective-permute-start.3 = (f32[2,104,128]{2,1,0:T(8,128)S(1)}, f32[2,104,128]{2,1,0:T(8,128)S(1)}, u32[]{:S(2)}, u32[]{:S(2)}) collective-permute-start(f32[2,104,128]{2,1,0:T(8,128)S(1)} %get-tuple-element.33), channel_id=1, source_target_pairs={{0,48},{8,56},{16,32},{24,40},{32,16},{40,24},{48,0},{56,8},{64,11... | collective-permute-start | bytes 319496 | tf_op jit(solution)/shard_map/ppermute | solution.py:306
  40.1 10.2 %collective-permute-start.4 = (f32[2,104,128]{2,1,0:T(8,128)S(1)}, f32[2,104,128]{2,1,0:T(8,128)S(1)}, u32[]{:S(2)}, u32[]{:S(2)}) collective-permute-start(f32[2,104,128]{2,1,0:T(8,128)S(1)} %get-tuple-element.34), channel_id=1, source_target_pairs={{0,32},{8,40},{16,48},{24,56},{32,0},{40,8},{48,16},{56,24},{64,96... | collective-permute-start | bytes 319496 | tf_op jit(solution)/shard_map/ppermute | solution.py:306
  51.4 14.2 %all-to-all-start.1 = ((f32[8,128,128]{2,1,0:T(8,128)}), f32[8,128,128]{2,1,0:T(8,128)S(1)}, u32[]{:S(2)}, u32[]{:S(2)}) async-start(f32[8,128,128]{2,1,0:T(8,128)} %memory_part.1), calls=%async_computation.1 | async-start | bytes 1048576 | tf_op jit(solution)/shard_map/all_to_all | solution.py:332
  56.4 9.2 %collective-permute-start.5 = (f32[104,128]{1,0:T(8,128)S(1)}, f32[104,128]{1,0:T(8,128)S(1)}, u32[]{:S(2)}, u32[]{:S(2)}) collective-permute-start(f32[104,128]{1,0:T(8,128)S(1)} %get-tuple-element.40), channel_id=1, source_target_pairs={{0,64},{8,72},{16,80},{24,88},{32,96},{40,104},{48,112},{56,120},{... | collective-permute-start | bytes 159752 | tf_op jit(solution)/shard_map/ppermute | solution.py:306

commit v4 on v3

--- a/solution.py
+++ b/solution.py
@@ -16,8 +16,11 @@
 SMALL = 128
 LARGE = 272
 TB = 256
-MEM_PARTS = 4
-ROW_PARTS = 4
+CH = 512
+ROW_PARTS = 2
+MEM_PARTS = 2
+AHEAD = 1
+CHUNK = 128 + 64 + 32 + 8
 f32 = jnp.float32
 bf16 = jnp.bfloat16
 
@@ -32,8 +35,9 @@
 
 def main_kernel(
     sidx, masked_hbm, q_hbm, g_hbm, mem_hbm, wq_hbm, wk_hbm, wv_hbm, wo_hbm,
-    keep_a, send_a, keep_b, send_b,
+    keep, send,
     masked, q_in, g_in, mem, qc, gc, kv, wkv, wq2, wo2, pos, off_v, off_s,
+    kvt, sc_s, dp_s, eb_s,
     dkv, wqo, wkv_out, wqo_out,
     mem_sem, row_sem, w_sem, off_sem,
 ):
@@ -50,11 +54,10 @@
         )
     ]
     mrows = LAT // MEM_PARTS
+    mem_parts = [pl.ds(i * mrows, mrows) for i in range(MEM_PARTS)]
     mem_copies = [
-        pltpu.make_async_copy(
-            mem_hbm.at[pl.ds(i * mrows, mrows)], mem.at[pl.ds(i * mrows, mrows)], mem_sem.at[i]
-        )
-        for i in range(MEM_PARTS)
+        pltpu.make_async_copy(mem_hbm.at[part], mem.at[part], mem_sem.at[i])
+        for i, part in enumerate(mem_parts)
     ]
     rrows = ROWS // ROW_PARTS
     row_copies = [
@@ -68,9 +71,7 @@
     ]
     mask_copy = pltpu.make_async_copy(masked_hbm, masked, off_sem)
     mask_copy.start()
-    for c in w_copies + mem_copies:
-        c.start()
-    for pair in row_copies:
+    for pair in row_copies[:AHEAD]:
         for c in pair:
             c.start()
 
@@ -96,15 +97,8 @@
     qc[pl.ds(0, 16), :] = jnp.zeros((16, E), bf16)
     gc[pl.ds(0, 16), :] = jnp.zeros((16, E), bf16)
 
-    for c in w_copies:
-        c.wait()
     wq2[DH:, :] = jnp.zeros((DH, E), bf16)
     wo2[:DH, :] = jnp.zeros((DH, E), bf16)
-    for i, c in enumerate(mem_copies):
-        c.wait()
-        part = pl.ds(i * mrows, mrows)
-        kv[part, :] = _dot(mem[part, :], wkv[...], NT).astype(bf16)
-
     off_copy.wait()
     total = off_s[32, 0]
 
@@ -125,8 +119,14 @@
     per = rrows // PACK
     for b in range(ROWS // PACK):
         if b % per == 0:
-            for c in row_copies[b // per]:
+            part = b // per
+            for c in row_copies[part]:
                 c.wait()
+            for c in row_copies[part + AHEAD] if part + AHEAD < ROW_PARTS else ():
+                c.start()
+            if part + AHEAD == ROW_PARTS:
+                for c in w_copies + mem_copies:
+                    c.start()
         base = off_s[2 * b, 0]
         nxt = off_s[2 * b + 2, 0]
         start = pl.multiple_of((base // 16) * 16, 16)
@@ -134,41 +134,84 @@
         pl.when(few)(functools.partial(put, b, start, SMALL))
         pl.when(jnp.logical_not(few))(functools.partial(put, b, start, LARGE))
 
+    for c in w_copies:
+        c.wait()
+    for c, part in zip(mem_copies, mem_parts):
+        c.wait()
+        proj = _dot(mem[part, :], wkv[...], NT)
+        kv[part, :] = proj.astype(bf16)
+        kvt[:, part] = proj.T.astype(bf16)
+
     tail = pl.ds(pl.multiple_of(((total + 15) // 16) * 16, 16), TB)
     qc[tail, :] = jnp.zeros((TB, E), bf16)
     gc[tail, :] = jnp.zeros((TB, E), bf16)
 
-    def block(i, _):
+    half = lax.broadcasted_iota(jnp.int32, (TB, 128), 1) < DH
+    none = jnp.zeros((DH, TB), bf16)
+    parts = [slice(c * CH, (c + 1) * CH) for c in range(LAT // CH)]
+
+    def fold(x, op):
+        rows = [x[8 * k : 8 * (k + 1)] for k in range(x.shape[0] // 8)]
+        while len(rows) > 1:
+            rows = [op(a, b) for a, b in zip(rows[::2], rows[1::2])]
+        return rows[0]
+
+    def begin(i):
         rows = pl.ds(pl.multiple_of(i * TB, TB), TB)
-        q = qc[rows, :]
-        g = gc[rows, :]
-        qp = _dot(q, wq2[...], NT).astype(bf16).astype(f32) * 0.125
-        da = _dot(g, wo2[...], NT).astype(bf16)
-        score = _dot(qp.astype(bf16), kv[...], NT)
-        dprob = _dot(da, kv[...], NT)
-        top = jnp.max(score, axis=1, keepdims=True)
-        e = jnp.exp(score - top)
-        inv = 1.0 / jnp.sum(e, axis=1, keepdims=True)
-        eb = e.astype(bf16)
-        att = (_dot(eb, kv[...], NN) * inv).astype(bf16)
-        daf = da.astype(f32)
-        delta = jnp.sum(daf * att.astype(f32), axis=1, keepdims=True)
-        ds = (e * (dprob - delta)).astype(bf16)
-        dq = _dot(ds, kv[...], NN) * (inv * 0.125)
-        lane = lax.broadcasted_iota(jnp.int32, (TB, 128), 1)
-        x = jnp.where(lane < DH, dq, att.astype(f32))
-        y = (qp + daf) * inv
-        xt = x.T.astype(bf16)
-        yt = y.T.astype(bf16)
-        wqo[:DH, :] += _dot(xt[:DH], q, NN)
-        wqo[DH:, :] += _dot(xt[DH:], g, NN)
-        dkv[:DH, :] += _dot(yt[:DH], ds, NN)
-        dkv[DH:, :] += _dot(yt[DH:], eb, NN)
-        return 0
-
-    lax.fori_loop(0, (total + TB - 1) // TB, block, 0)
-
-    wkvt = _dot(dkv[...].astype(bf16), mem[...], NN)
+        qp = _dot(qc[rows, :], wq2[...], NT).astype(bf16).astype(f32) * 0.125
+        da = _dot(gc[rows, :], wo2[...], NT).astype(bf16).astype(f32)
+        zt = (qp + da).T
+        qt = jnp.concatenate([zt[:DH].astype(bf16), none], axis=0)
+        gt = jnp.concatenate([none, zt[DH:].astype(bf16)], axis=0)
+        return zt, qt, gt
+
+    def scores(qt, part):
+        score = _dot(kv[part, :], qt, NN)
+        sc_s[part, :] = score
+        return fold(score, jnp.maximum)
+
+    def over(op, a, b):
+        return b if a is None else op(a, b)
+
+    zt0, qt0, gt0 = begin(0)
+    top0 = None
+    for part in parts:
+        top0 = over(jnp.maximum, top0, scores(qt0, part))
+        dp_s[part, :] = _dot(kv[part, :], gt0, NN)
+
+    def block(i, carried):
+        zt, top = carried
+        zt_n, qt_n, gt_n = begin(i + 1)
+        top = jnp.max(top, axis=0, keepdims=True)
+        norm = att = dq = top_n = None
+        for part in parts:
+            e = jnp.exp(sc_s[part, :] - top)
+            eb = e.astype(bf16)
+            eb_s[part, :] = eb
+            norm = over(jnp.add, norm, fold(e, jnp.add))
+            att = over(jnp.add, att, _dot(kvt[DH:, part], eb, NN))
+            top_n = over(jnp.maximum, top_n, scores(qt_n, part))
+        inv = 1.0 / jnp.sum(norm, axis=0, keepdims=True)
+        att = (att * inv).astype(bf16).astype(f32)
+        delta = jnp.sum(zt[DH:] * att, axis=0, keepdims=True)
+        y = (zt * inv).T
+        yk = jnp.where(half, y, 0.0).astype(bf16)
+        yv = jnp.where(half, 0.0, y).astype(bf16)
+        for part in parts:
+            eb = eb_s[part, :]
+            ds = (eb.astype(f32) * (dp_s[part, :] - delta)).astype(bf16)
+            dp_s[part, :] = _dot(kv[part, :], gt_n, NN)
+            dq = over(jnp.add, dq, _dot(kvt[:DH, part], ds, NN))
+            dkv[part, :] += _dot(ds, yk, NN) + _dot(eb, yv, NN)
+        rows = pl.ds(pl.multiple_of(i * TB, TB), TB)
+        xq = (dq * (inv * 0.125)).astype(bf16)
+        wqo[:DH, :] += _dot(xq, qc[rows, :], NN)
+        wqo[DH:, :] += _dot(att.astype(bf16), gc[rows, :], NN)
+        return zt_n, top_n
+
+    lax.fori_loop(0, (total + TB - 1) // TB, block, (zt0, top0))
+
+    wkvt = _dot(dkv[...].T.astype(bf16), mem[...], NN)
     lane64 = lax.broadcasted_iota(jnp.int32, (64, 128), 1)
     for t in range(8):
         tk = wkvt[:DH, 128 * t : 128 * (t + 1)]
@@ -190,15 +233,12 @@
     core = me & 1
     for p in range(16):
         i, rc = p % 8, p // 8
-        z, x = i // 4, i % 4
-        a = (keep_a, send_a)[rc]
-        b = (keep_b, send_b)[rc]
-        s = z * 8 + x * 2 + (core ^ rc)
-        a[i] = dkv[:, pl.ds(pl.multiple_of(s * 128, 128), 128)]
-        s = me ^ (z * 8 + x * 2 + rc)
-        b[i, 0:64] = wkv_out[s]
-        b[i, 64:96] = wqo_out[s]
-        b[i, 96:104] = count
+        out = (keep, send)[rc]
+        s = (i // 4) * 8 + (i % 4) * 2 + (core ^ rc)
+        out[i, 0:128] = dkv[pl.ds(pl.multiple_of(s * 128, 128), 128), :]
+        out[i, 128:192] = wkv_out[s]
+        out[i, 192:224] = wqo_out[s]
+        out[i, 224:232] = count
 
 
 def in_hbm(x):
@@ -212,15 +252,14 @@
 def run_main(sidx, masked, queries, grads, memory, w_query, w_key, w_value, w_out):
     any_ = pl.BlockSpec(memory_space=pl.ANY)
     vm = pl.BlockSpec(memory_space=pltpu.VMEM)
-    a = pltpu.VMEM((8, 128, 128), f32)
-    b = pltpu.VMEM((8, 104, 128), f32)
+    a = pltpu.VMEM((8, CHUNK, 128), f32)
     arrays = [in_hbm(x) for x in (queries, grads, memory, w_query, w_key, w_value, w_out)]
     pad = ROWS + LARGE + TB
     return pl.pallas_call(
         main_kernel,
-        out_shape=(a, a, b, b),
+        out_shape=(a, a),
         in_specs=[pl.BlockSpec(memory_space=pltpu.SMEM)] + [any_] * 8,
-        out_specs=(vm,) * 4,
+        out_specs=(vm,) * 2,
         scratch_shapes=[
             pltpu.VMEM((32, 128), jnp.int32),
             pltpu.VMEM((ROWS, E), bf16),
@@ -235,7 +274,11 @@
             pltpu.VMEM((32, 128), jnp.int32),
             pltpu.VMEM((40, 128), jnp.int32),
             pltpu.SMEM((40, 128), jnp.int32),
-            pltpu.VMEM((128, LAT), f32),
+            pltpu.VMEM((128, LAT), bf16),
+            pltpu.VMEM((LAT, TB), f32),
+            pltpu.VMEM((LAT, TB), f32),
+            pltpu.VMEM((LAT, TB), bf16),
+            pltpu.VMEM((LAT, 128), f32),
             pltpu.VMEM((128, E), f32),
             pltpu.VMEM((16, 64, 128), f32),
             pltpu.VMEM((16, 32, 128), f32),
@@ -250,55 +293,71 @@
     )(sidx, in_hbm(masked), *arrays)
 
 
-def head_kernel(parts, wk, wv, out):
-    d = parts[0]
-    for k in range(1, 8):
-        d = d + parts[k]
-    dt = d.T.astype(bf16)
+VM = pl.BlockSpec(memory_space=pltpu.VMEM)
+
+
+def total_of(parts, rows):
+    t = parts[0, rows]
+    for k in range(1, parts.shape[0]):
+        t = t + parts[k, rows]
+    return t
+
+
+def head_kernel(parts, wk, wv, out, rest):
+    dt = total_of(parts, slice(0, 128)).astype(bf16)
     for c in range(8):
         cols = slice(128 * c, 128 * (c + 1))
         w = jnp.concatenate([wk[:, cols], wv[:, cols]], axis=0)
         out[c] = _dot(dt, w, NN)
+    rest[...] = total_of(parts, slice(128, CHUNK))
 
 
 def run_head(parts, wk_t, wv_t):
-    vm = pl.BlockSpec(memory_space=pltpu.VMEM)
     return pl.pallas_call(
         head_kernel,
-        out_shape=pltpu.VMEM((8, 128, 128), f32),
-        in_specs=[vm] * 3,
-        out_specs=vm,
+        out_shape=(pltpu.VMEM((8, 128, 128), f32), pltpu.VMEM((CHUNK - 128, 128), f32)),
+        in_specs=[VM] * 3,
+        out_specs=(VM,) * 2,
         name="memory_part",
     )(in_vmem(parts), in_vmem(wk_t), in_vmem(wv_t))
 
 
-def last_kernel(mine, got, parts, gwq, gwk, gwv, gwo_t, gmem):
-    b = mine[...] + got[...]
-    scale = 1.0 / b[96:97, :]
-    b = b * scale
+def weights_kernel(rest, gwq, gwk, gwv, gwo_t, scale_out):
+    scale = 1.0 / rest[96:104, :]
+    scale_out[...] = scale
+    b = rest[0:96] * scale[0:1]
     kv_t = b[0:64].T
     gwk[...] = kv_t[:64]
     gwv[...] = kv_t[64:]
     qo_t = b[64:96].T
     gwq[...] = jnp.concatenate([qo_t[0:32], qo_t[64:96]], axis=1)
     gwo_t[...] = jnp.concatenate([qo_t[32:64], qo_t[96:128]], axis=1)
-    m = parts[0]
-    for k in range(1, 8):
-        m = m + parts[k]
-    gmem[...] = m * scale
-
-
-def run_last(mine, got, parts):
-    vm = pl.BlockSpec(memory_space=pltpu.VMEM)
+
+
+def run_weights(rest):
     small = jax.ShapeDtypeStruct((32, 64), f32)
     square = jax.ShapeDtypeStruct((64, 64), f32)
     return pl.pallas_call(
+        weights_kernel,
+        out_shape=(small, square, square, small, pltpu.VMEM((8, 128), f32)),
+        in_specs=[VM],
+        out_specs=(VM,) * 5,
+        name="weight_parts",
+    )(in_vmem(rest))
+
+
+def last_kernel(parts, scale, gmem):
+    gmem[...] = total_of(parts, slice(0, 128)) * scale[0:1]
+
+
+def run_last(parts, scale):
+    return pl.pallas_call(
         last_kernel,
-        out_shape=(small, square, square, small, jax.ShapeDtypeStruct((128, 128), f32)),
-        in_specs=[vm] * 3,
-        out_specs=(vm,) * 5,
-        name="gradients",
-    )(in_vmem(mine), in_vmem(got), in_vmem(parts))
+        out_shape=jax.ShapeDtypeStruct((128, 128), f32),
+        in_specs=[VM] * 2,
+        out_specs=VM,
+        name="grad_memory",
+    )(in_vmem(parts), in_vmem(scale))
 
 
 def swap(x, axis, bits):
@@ -306,31 +365,17 @@
     return lax.ppermute(x, axis, [(i, i ^ bits) for i in range(n)])
 
 
-hold = lax.optimization_barrier
-
-
 def shards(queries, memory, w_query, w_key, w_value, w_out, grad_out, masked):
     seq = lax.axis_index("seq").astype(jnp.int32).reshape(1)
     wk_t, wv_t = w_key.T, w_value.T
-    keep_a, send_a, keep_b, send_b = run_main(
+    keep, send = run_main(
         seq, masked.reshape(32, 128), queries, grad_out, memory, w_query.T, wk_t, wv_t, w_out
     )
-    got_a = swap(send_a, "seq", 1)
-    got_b = swap(send_b, "seq", 1)
     groups = [[z * 8 + x * 2 + core for z in range(2) for x in range(4)] for core in range(2)]
-    sum_a, sum_b = hold((keep_a + got_a, keep_b + got_b))
-    sum_b = sum_b.reshape(2, 4, 104, 128)
-    sends = hold((sum_b[:, 1], sum_b[:, 3], sum_b[:, 2]))
-    ins = [swap(x, "seq", bits) for x, bits in zip(sends, (2, 6, 4))]
-    parts = lax.all_to_all(sum_a, "seq", 0, 0, axis_index_groups=groups)
-    parts, ins = hold((parts, ins))
-    part = run_head(parts, wk_t, wv_t)
-
-    sum_b = sum_b[:, 0] + ins[0] + ins[1] + ins[2]
-    part, mine, send = hold((part, sum_b[0], sum_b[1]))
-    got = swap(send, "seq", 8)
-    parts = lax.all_to_all(part, "head", 0, 0)
-    grad_wq, grad_wk, grad_wv, grad_wo_t, grad_memory = run_last(mine, got, parts)
+    parts = lax.all_to_all(keep + swap(send, "seq", 1), "seq", 0, 0, axis_index_groups=groups)
+    part, rest = run_head(parts, wk_t, wv_t)
+    grad_wq, grad_wk, grad_wv, grad_wo_t, scale = run_weights(rest)
+    grad_memory = run_last(lax.all_to_all(part, "head", 0, 0), scale)
     return (grad_wq, grad_wk, grad_wv, grad_wo_t.T, grad_memory)
 
 

time: 67.3 us -> 65.1 us (0.967)
  blocking collectives: 0 us -> 29.9 us
  starting transfers between devices: 28.8 us -> 5.01 us
  waiting for transfers between devices: 17.3 us -> 11.2 us
  Pallas kernels: 18.7 us -> 17.6 us
  other arithmetic: 0.92 us -> 0.1 us
    all_to_all x0 -> x1, blocking collectives: none -> 29.9 us  [shards(): lax.all_to_all(keep + swap(send, 'seq', 1), 'seq', 0, 0, axis_index_group...]
    all_to_all x2 -> x1, starting transfers between devices: 19.8 us -> 4.92 us  [shards(): grad_memory = run_last(lax.all_to_all(part, 'head', 0, 0), scale)]
    ppermute x6 -> x1, waiting for transfers between devices: 17.2 us -> 2.51 us  [swap(): return lax.ppermute(x, axis, [(i, i ^ bits) for i in range(n)])]
    ppermute x6 -> x1, starting transfers between devices: 8.93 us -> 0.09 us  [swap(): return lax.ppermute(x, axis, [(i, i ^ bits) for i in range(n)])]
    all_to_all x2 -> x1, waiting for transfers between devices: 0.12 us -> 8.69 us  [shards(): grad_memory = run_last(lax.all_to_all(part, 'head', 0, 0), scale)]
    pallas_call x3 -> x4, Pallas kernels: 18.7 us -> 17.6 us  [the longest x1 15.2 us: run_main(): pl.pallas_call(main_kernel, out_shape=(a, a), in_specs=[pl.BlockSpec(memo...]
    add x3 -> x1, other arithmetic: 0.92 us -> 0.1 us  [shards(): keep + swap(send, 'seq', 1)]
  transfers between devices with their start and end apart: 8 -> 2, of which waited for: 6 -> 2; matrix products, arithmetic and copies ran while one was open for 0% -> 0% of each run, Pallas kernels for 0% -> 1%
where the time goes in v4:
time: 65.1 us; the launch traced here: 64.5 us
  blocking collectives  29.9 us (46%)
  Pallas kernels  17.6 us (27%)
  waiting for transfers between devices  11.2 us (17%)
  starting transfers between devices  5.01 us (8%)
  between operations  0.68 us (1%)
    all_to_all x1, blocking collectives, shards(): lax.all_to_all(keep + swap(send, 'seq', 1), 'seq', 0, 0, axis_index_group...  29.9 us
    pallas_call x1, Pallas kernels, run_main(): pl.pallas_call(main_kernel, out_shape=(a, a), in_specs=[pl.BlockSpec(memo...  15.2 us
    all_to_all x1, waiting for transfers between devices, shards(): grad_memory = run_last(lax.all_to_all(part, 'head', 0, 0), scale)  8.69 us
    all_to_all x1, starting transfers between devices, shards(): grad_memory = run_last(lax.all_to_all(part, 'head', 0, 0), scale)  4.92 us
    ppermute x1, waiting for transfers between devices, swap(): return lax.ppermute(x, axis, [(i, i ^ bits) for i in range(n)])  2.51 us
  transfers between devices with their start and end apart: 2, of which 2 were waited for; matrix products, arithmetic and copies ran while one was open for 0% of the time, Pallas kernels for 1%

profile of v4, /device:TPU:0, one launch (start us, length us, event | category | flops | bytes accessed | tf_op | source)
XLA Modules:
  0.0 64.5 jit_solution(18325136728480659648)
XLA Ops:
  0.6 15.2 %masked_rows.1 = (f32[8,232,128]{2,1,0:T(8,128)S(1)}, f32[8,232,128]{2,1,0:T(8,128)S(1)}) custom-call(s32[1]{0:T(128)} %bitcast.sidx, s32[32,128]{1,0:T(8,128)} %bitcast.11, bf16[4096,512]{1,0:T(8,128)(2,1)} %q_hbm.1, bf16[4096,512]{1,0:T(8,128)(2,1)} %g_hbm.1, bf16[2048,1024]{1,0:T(8,128)(2,1)} %mem_hbm.1, bf16[64,512]{1,0:T(8,128)(2,1)} %bitcast.10, ...), custom_call_target="tpu_custom_call" | custom-call | flops 10000000000 | bytes 14680064 | tf_op jit(solution)/shard_map/masked_rows/pallas_call | solution.py:258
  15.8 0.0 copy-start
  15.8 0.0 copy-start.1
  15.8 0.1 collective-permute-start
  15.9 2.5 %collective-permute-done = f32[8,232,128]{2,1,0:T(8,128)S(1)} collective-permute-done((f32[8,232,128]{2,1,0:T(8,128)S(1)}, f32[8,232,128]{2,1,0:T(8,128)S(1)}, u32[]{:S(2)}, u32[]{:S(2)}) %collective-permute-start) | collective-permute-done | bytes 950304 | tf_op jit(solution)/shard_map/ppermute | solution.py:365
  18.4 0.1 add.3
  18.5 29.9 %all_to_all.10.parts = f32[8,232,128]{2,1,0:T(8,128)S(1)} all-to-all(f32[8,232,128]{2,1,0:T(8,128)S(1)} %add.3), channel_id=1, replica_groups={{0,16,32,48,64,80,96,112},{8,24,40,56,72,88,104,120},{1,17,33,49,65,81,..., dimensions={0} | all-to-all | bytes 1900544 | tf_op jit(solution)/shard_map/all_to_all | solution.py:375
  48.5 0.0 copy-done
  48.5 0.0 copy-done.1
  48.5 1.0 %memory_part.1 = (f32[8,128,128]{2,1,0:T(8,128)}, f32[104,128]{1,0:T(8,128)S(1)}) custom-call(f32[8,232,128]{2,1,0:T(8,128)S(1)} %all_to_all.10.parts, bf16[64,1024]{1,0:T(8,128)(2,1)S(1)} %bitcast.7, bf16[64,1024]{1,0:T(8,128)(2,1)S(1)} %bitcast.9), custom_call_target="tpu_custom_call" | custom-call | tf_op jit(solution)/shard_map/memory_part/pallas_call | solution.py:316
  49.5 4.9 %all-to-all-start.1 = ((f32[8,128,128]{2,1,0:T(8,128)}), f32[8,128,128]{2,1,0:T(8,128)S(1)}, u32[]{:S(2)}, u32[]{:S(2)}) async-start(f32[8,128,128]{2,1,0:T(8,128)} %get-tuple-element.21), calls=%async_computation.1 | async-start | bytes 1048576 | tf_op jit(solution)/shard_map/all_to_all | solution.py:378
  54.4 0.8 %weight_parts.1 = (f32[32,64]{1,0:T(8,128)}, f32[64,64]{1,0:T(8,128)}, f32[64,64]{1,0:T(8,128)}, f32[32,64]{1,0:T(8,128)}, f32[8,128]{1,0:T(8,128)S(1)}) custom-call(f32[104,128]{1,0:T(8,128)S(1)} %get-tuple-element.16.rest), custom_call_target="tpu_custom_call" | custom-call | tf_op jit(solution)/shard_map/weight_parts/pallas_call | solution.py:340
  55.2 8.7 %all-to-all-done.1.parts = f32[8,128,128]{2,1,0:T(8,128)S(1)} async-done(((f32[8,128,128]{2,1,0:T(8,128)}), f32[8,128,128]{2,1,0:T(8,128)S(1)}, u32[]{:S(2)}, u32[]{:S(2)}) %all-to-all-start.1) | async-done | bytes 524320 | tf_op jit(solution)/shard_map/all_to_all | solution.py:378
  63.9 0.7 %grad_memory.1 = f32[128,128]{1,0:T(8,128)} custom-call(f32[8,128,128]{2,1,0:T(8,128)S(1)} %all-to-all-done.1.parts, f32[8,128]{1,0:T(8,128)S(1)} %get-tuple-element.22.scale), custom_call_target="tpu_custom_call" | custom-call | tf_op jit(solution)/shard_map/grad_memory/pallas_call | solution.py:354
Async XLA Ops:
  15.8 32.7 %copy-start = (bf16[1024,64]{0,1:T(8,128)(2,1)S(1)}, bf16[1024,64]{0,1:T(8,128)(2,1)}, u32[]{:S(2)}) copy-start(bf16[1024,64]{0,1:T(8,128)(2,1)} %param.11) | copy-start | bytes 393220
  15.8 32.7 %copy-start.1 = (bf16[1024,64]{0,1:T(8,128)(2,1)S(1)}, bf16[1024,64]{0,1:T(8,128)(2,1)}, u32[]{:S(2)}) copy-start(bf16[1024,64]{0,1:T(8,128)(2,1)} %param.12) | copy-start | bytes 393220
  15.8 2.6 %collective-permute-start = (f32[8,232,128]{2,1,0:T(8,128)S(1)}, f32[8,232,128]{2,1,0:T(8,128)S(1)}, u32[]{:S(2)}, u32[]{:S(2)}) collective-permute-start(f32[8,232,128]{2,1,0:T(8,128)S(1)} %get-tuple-element.15), channel_id=1, source_target_pairs={{0,8},{8,0},{16,24},{24,16},{32,40},{40,32},{48,56},{56,48},{64,72... | collective-permute-start | bytes 2850824 | tf_op jit(solution)/shard_map/ppermute | solution.py:365
  49.5 14.4 %all-to-all-start.1 = ((f32[8,128,128]{2,1,0:T(8,128)}), f32[8,128,128]{2,1,0:T(8,128)S(1)}, u32[]{:S(2)}, u32[]{:S(2)}) async-start(f32[8,128,128]{2,1,0:T(8,128)} %get-tuple-element.21), calls=%async_computation.1 | async-start | bytes 1048576 | tf_op jit(solution)/shard_map/all_to_all | solution.py:378

commit v5 on v4

--- a/solution.py
+++ b/solution.py
@@ -16,10 +16,9 @@
 SMALL = 128
 LARGE = 272
 TB = 256
-CH = 512
-ROW_PARTS = 2
-MEM_PARTS = 2
-AHEAD = 1
+CH = 1024
+ROW_PARTS = 4
+MEM_PARTS = 4
 CHUNK = 128 + 64 + 32 + 8
 f32 = jnp.float32
 bf16 = jnp.bfloat16
@@ -71,9 +70,8 @@
     ]
     mask_copy = pltpu.make_async_copy(masked_hbm, masked, off_sem)
     mask_copy.start()
-    for pair in row_copies[:AHEAD]:
-        for c in pair:
-            c.start()
+    for c in w_copies[:2] + mem_copies + row_copies[0] + w_copies[2:]:
+        c.start()
 
     mask_copy.wait()
     ones = masked[...].astype(f32)
@@ -99,6 +97,18 @@
 
     wq2[DH:, :] = jnp.zeros((DH, E), bf16)
     wo2[:DH, :] = jnp.zeros((DH, E), bf16)
+    for c in w_copies:
+        c.wait()
+    for i, c in enumerate(mem_copies):
+        c.wait()
+        if i == 0:
+            for pair in row_copies[1:]:
+                for later in pair:
+                    later.start()
+    for part in mem_parts:
+        proj = _dot(mem[part, :], wkv[...], NT)
+        kv[part, :] = proj.astype(bf16)
+        kvt[:, part] = proj.T.astype(bf16)
     off_copy.wait()
     total = off_s[32, 0]
 
@@ -117,30 +127,28 @@
             d_ref[rest, :] = rows[16:].astype(bf16)
 
     per = rrows // PACK
-    for b in range(ROWS // PACK):
-        if b % per == 0:
-            part = b // per
-            for c in row_copies[part]:
-                c.wait()
-            for c in row_copies[part + AHEAD] if part + AHEAD < ROW_PARTS else ():
-                c.start()
-            if part + AHEAD == ROW_PARTS:
-                for c in w_copies + mem_copies:
-                    c.start()
+
+    def place(b):
         base = off_s[2 * b, 0]
-        nxt = off_s[2 * b + 2, 0]
         start = pl.multiple_of((base // 16) * 16, 16)
-        few = nxt - start < SMALL
-        pl.when(few)(functools.partial(put, b, start, SMALL))
-        pl.when(jnp.logical_not(few))(functools.partial(put, b, start, LARGE))
-
-    for c in w_copies:
-        c.wait()
-    for c, part in zip(mem_copies, mem_parts):
-        c.wait()
-        proj = _dot(mem[part, :], wkv[...], NT)
-        kv[part, :] = proj.astype(bf16)
-        kvt[:, part] = proj.T.astype(bf16)
+        return start, off_s[2 * b + 2, 0] - start < SMALL
+
+    for part, pair in enumerate(row_copies):
+        for c in pair:
+            c.wait()
+        blocks = [(b, *place(b)) for b in range(part * per, (part + 1) * per)]
+        few = functools.reduce(jnp.logical_and, [ok for _, _, ok in blocks])
+
+        def small():
+            for b, start, _ in blocks:
+                put(b, start, SMALL)
+
+        def large():
+            for b, start, _ in blocks:
+                put(b, start, LARGE)
+
+        pl.when(few)(small)
+        pl.when(jnp.logical_not(few))(large)
 
     tail = pl.ds(pl.multiple_of(((total + 15) // 16) * 16, 16), TB)
     qc[tail, :] = jnp.zeros((TB, E), bf16)
@@ -179,9 +187,9 @@
         top0 = over(jnp.maximum, top0, scores(qt0, part))
         dp_s[part, :] = _dot(kv[part, :], gt0, NN)
 
-    def block(i, carried):
+    def block(i, carried, more=True):
         zt, top = carried
-        zt_n, qt_n, gt_n = begin(i + 1)
+        zt_n, qt_n, gt_n = begin(i + 1) if more else (None, None, None)
         top = jnp.max(top, axis=0, keepdims=True)
         norm = att = dq = top_n = None
         for part in parts:
@@ -190,26 +198,30 @@
             eb_s[part, :] = eb
             norm = over(jnp.add, norm, fold(e, jnp.add))
             att = over(jnp.add, att, _dot(kvt[DH:, part], eb, NN))
-            top_n = over(jnp.maximum, top_n, scores(qt_n, part))
+            if more:
+                top_n = over(jnp.maximum, top_n, scores(qt_n, part))
         inv = 1.0 / jnp.sum(norm, axis=0, keepdims=True)
         att = (att * inv).astype(bf16).astype(f32)
         delta = jnp.sum(zt[DH:] * att, axis=0, keepdims=True)
         y = (zt * inv).T
         yk = jnp.where(half, y, 0.0).astype(bf16)
         yv = jnp.where(half, 0.0, y).astype(bf16)
+        ykv = jnp.concatenate([yk, yv], axis=0)
         for part in parts:
             eb = eb_s[part, :]
             ds = (eb.astype(f32) * (dp_s[part, :] - delta)).astype(bf16)
-            dp_s[part, :] = _dot(kv[part, :], gt_n, NN)
+            if more:
+                dp_s[part, :] = _dot(kv[part, :], gt_n, NN)
             dq = over(jnp.add, dq, _dot(kvt[:DH, part], ds, NN))
-            dkv[part, :] += _dot(ds, yk, NN) + _dot(eb, yv, NN)
+            dkv[part, :] += _dot(jnp.concatenate([ds, eb], axis=1), ykv, NN)
         rows = pl.ds(pl.multiple_of(i * TB, TB), TB)
         xq = (dq * (inv * 0.125)).astype(bf16)
         wqo[:DH, :] += _dot(xq, qc[rows, :], NN)
         wqo[DH:, :] += _dot(att.astype(bf16), gc[rows, :], NN)
         return zt_n, top_n
 
-    lax.fori_loop(0, (total + TB - 1) // TB, block, (zt0, top0))
+    last = jnp.maximum((total + TB - 1) // TB - 1, 0)
+    block(last, lax.fori_loop(0, last, block, (zt0, top0)), False)
 
     wkvt = _dot(dkv[...].T.astype(bf16), mem[...], NN)
     lane64 = lax.broadcasted_iota(jnp.int32, (64, 128), 1)

time: 65.1 us -> 61.8 us (0.949)
  Pallas kernels: 17.6 us -> 14.3 us
    pallas_call x1, Pallas kernels: 15.2 us -> 11.8 us  [run_main(): pl.pallas_call(main_kernel, out_shape=(a, a), in_specs=[pl.BlockSpec(memo...]
where the time goes in v5:
time: 61.8 us; the launch traced here: 61.2 us
  blocking collectives  29.9 us (48%)
  Pallas kernels  14.3 us (23%)
  waiting for transfers between devices  11.2 us (18%)
  starting transfers between devices  5 us (8%)
  between operations  0.68 us (1%)
    all_to_all x1, blocking collectives, shards(): lax.all_to_all(keep + swap(send, 'seq', 1), 'seq', 0, 0, axis_index_group...  29.9 us
    pallas_call x1, Pallas kernels, run_main(): pl.pallas_call(main_kernel, out_shape=(a, a), in_specs=[pl.BlockSpec(memo...  11.8 us
    all_to_all x1, waiting for transfers between devices, shards(): grad_memory = run_last(lax.all_to_all(part, 'head', 0, 0), scale)  8.69 us
    all_to_all x1, starting transfers between devices, shards(): grad_memory = run_last(lax.all_to_all(part, 'head', 0, 0), scale)  4.91 us
    ppermute x1, waiting for transfers between devices, swap(): return lax.ppermute(x, axis, [(i, i ^ bits) for i in range(n)])  2.51 us
  transfers between devices with their start and end apart: 2, of which 2 were waited for; matrix products, arithmetic and copies ran while one was open for 0% of the time, Pallas kernels for 1%

profile of v5, /device:TPU:0, one launch (start us, length us, event | category | flops | bytes accessed | tf_op | source)
XLA Modules:
  0.0 61.2 jit_solution(15316474752917741281)
XLA Ops:
  0.6 11.8 %masked_rows.1 = (f32[8,232,128]{2,1,0:T(8,128)S(1)}, f32[8,232,128]{2,1,0:T(8,128)S(1)}) custom-call(s32[1]{0:T(128)} %bitcast.sidx, s32[32,128]{1,0:T(8,128)} %bitcast.11, bf16[4096,512]{1,0:T(8,128)(2,1)} %q_hbm.1, bf16[4096,512]{1,0:T(8,128)(2,1)} %g_hbm.1, bf16[2048,1024]{1,0:T(8,128)(2,1)} %mem_hbm.1, bf16[64,512]{1,0:T(8,128)(2,1)} %bitcast.10, ...), custom_call_target="tpu_custom_call" | custom-call | flops 10000000000 | bytes 14680064 | tf_op jit(solution)/shard_map/masked_rows/pallas_call | solution.py:270
  12.5 0.0 copy-start
  12.5 0.0 copy-start.1
  12.5 0.1 collective-permute-start
  12.6 2.5 %collective-permute-done = f32[8,232,128]{2,1,0:T(8,128)S(1)} collective-permute-done((f32[8,232,128]{2,1,0:T(8,128)S(1)}, f32[8,232,128]{2,1,0:T(8,128)S(1)}, u32[]{:S(2)}, u32[]{:S(2)}) %collective-permute-start) | collective-permute-done | bytes 950304 | tf_op jit(solution)/shard_map/ppermute | solution.py:377
  15.1 0.1 add.3
  15.2 29.9 %all_to_all.10.parts = f32[8,232,128]{2,1,0:T(8,128)S(1)} all-to-all(f32[8,232,128]{2,1,0:T(8,128)S(1)} %add.3), channel_id=1, replica_groups={{0,16,32,48,64,80,96,112},{8,24,40,56,72,88,104,120},{1,17,33,49,65,81,..., dimensions={0} | all-to-all | bytes 1900544 | tf_op jit(solution)/shard_map/all_to_all | solution.py:387
  45.1 0.0 copy-done
  45.1 0.0 copy-done.1
  45.1 1.0 %memory_part.1 = (f32[8,128,128]{2,1,0:T(8,128)}, f32[104,128]{1,0:T(8,128)S(1)}) custom-call(f32[8,232,128]{2,1,0:T(8,128)S(1)} %all_to_all.10.parts, bf16[64,1024]{1,0:T(8,128)(2,1)S(1)} %bitcast.7, bf16[64,1024]{1,0:T(8,128)(2,1)S(1)} %bitcast.9), custom_call_target="tpu_custom_call" | custom-call | tf_op jit(solution)/shard_map/memory_part/pallas_call | solution.py:328
  46.2 4.9 %all-to-all-start.1 = ((f32[8,128,128]{2,1,0:T(8,128)}), f32[8,128,128]{2,1,0:T(8,128)S(1)}, u32[]{:S(2)}, u32[]{:S(2)}) async-start(f32[8,128,128]{2,1,0:T(8,128)} %get-tuple-element.21), calls=%async_computation.1 | async-start | bytes 1048576 | tf_op jit(solution)/shard_map/all_to_all | solution.py:390
  51.1 0.8 %weight_parts.1 = (f32[32,64]{1,0:T(8,128)}, f32[64,64]{1,0:T(8,128)}, f32[64,64]{1,0:T(8,128)}, f32[32,64]{1,0:T(8,128)}, f32[8,128]{1,0:T(8,128)S(1)}) custom-call(f32[104,128]{1,0:T(8,128)S(1)} %get-tuple-element.16.rest), custom_call_target="tpu_custom_call" | custom-call | tf_op jit(solution)/shard_map/weight_parts/pallas_call | solution.py:352
  51.8 8.7 %all-to-all-done.1.parts = f32[8,128,128]{2,1,0:T(8,128)S(1)} async-done(((f32[8,128,128]{2,1,0:T(8,128)}), f32[8,128,128]{2,1,0:T(8,128)S(1)}, u32[]{:S(2)}, u32[]{:S(2)}) %all-to-all-start.1) | async-done | bytes 524320 | tf_op jit(solution)/shard_map/all_to_all | solution.py:390
  60.5 0.7 %grad_memory.1 = f32[128,128]{1,0:T(8,128)} custom-call(f32[8,128,128]{2,1,0:T(8,128)S(1)} %all-to-all-done.1.parts, f32[8,128]{1,0:T(8,128)S(1)} %get-tuple-element.22.scale), custom_call_target="tpu_custom_call" | custom-call | tf_op jit(solution)/shard_map/grad_memory/pallas_call | solution.py:366
Async XLA Ops:
  12.5 32.6 %copy-start = (bf16[1024,64]{0,1:T(8,128)(2,1)S(1)}, bf16[1024,64]{0,1:T(8,128)(2,1)}, u32[]{:S(2)}) copy-start(bf16[1024,64]{0,1:T(8,128)(2,1)} %param.11) | copy-start | bytes 393220
  12.5 32.6 %copy-start.1 = (bf16[1024,64]{0,1:T(8,128)(2,1)S(1)}, bf16[1024,64]{0,1:T(8,128)(2,1)}, u32[]{:S(2)}) copy-start(bf16[1024,64]{0,1:T(8,128)(2,1)} %param.12) | copy-start | bytes 393220
  12.5 2.6 %collective-permute-start = (f32[8,232,128]{2,1,0:T(8,128)S(1)}, f32[8,232,128]{2,1,0:T(8,128)S(1)}, u32[]{:S(2)}, u32[]{:S(2)}) collective-permute-start(f32[8,232,128]{2,1,0:T(8,128)S(1)} %get-tuple-element.15), channel_id=1, source_target_pairs={{0,8},{8,0},{16,24},{24,16},{32,40},{40,32},{48,56},{56,48},{64,72... | collective-permute-start | bytes 2850824 | tf_op jit(solution)/shard_map/ppermute | solution.py:377
  46.2 14.4 %all-to-all-start.1 = ((f32[8,128,128]{2,1,0:T(8,128)}), f32[8,128,128]{2,1,0:T(8,128)S(1)}, u32[]{:S(2)}, u32[]{:S(2)}) async-start(f32[8,128,128]{2,1,0:T(8,128)} %get-tuple-element.21), calls=%async_computation.1 | async-start | bytes 1048576 | tf_op jit(solution)/shard_map/all_to_all | solution.py:390

commit v6 on v5

--- a/solution.py
+++ b/solution.py
@@ -16,7 +16,7 @@
 SMALL = 128
 LARGE = 272
 TB = 256
-CH = 1024
+CH = 256
 ROW_PARTS = 4
 MEM_PARTS = 4
 CHUNK = 128 + 64 + 32 + 8
@@ -47,8 +47,8 @@
             (
                 (wk_hbm, wkv.at[pl.ds(0, DH)]),
                 (wv_hbm, wkv.at[pl.ds(DH, DH)]),
-                (wq_hbm, wq2.at[pl.ds(0, DH)]),
-                (wo_hbm, wo2.at[pl.ds(DH, DH)]),
+                (wq_hbm, wq2),
+                (wo_hbm, wo2),
             )
         )
     ]
@@ -95,8 +95,6 @@
     qc[pl.ds(0, 16), :] = jnp.zeros((16, E), bf16)
     gc[pl.ds(0, 16), :] = jnp.zeros((16, E), bf16)
 
-    wq2[DH:, :] = jnp.zeros((DH, E), bf16)
-    wo2[:DH, :] = jnp.zeros((DH, E), bf16)
     for c in w_copies:
         c.wait()
     for i, c in enumerate(mem_copies):
@@ -166,11 +164,11 @@
 
     def begin(i):
         rows = pl.ds(pl.multiple_of(i * TB, TB), TB)
-        qp = _dot(qc[rows, :], wq2[...], NT).astype(bf16).astype(f32) * 0.125
-        da = _dot(gc[rows, :], wo2[...], NT).astype(bf16).astype(f32)
-        zt = (qp + da).T
-        qt = jnp.concatenate([zt[:DH].astype(bf16), none], axis=0)
-        gt = jnp.concatenate([none, zt[DH:].astype(bf16)], axis=0)
+        qt = (_dot(wq2[...], qc[rows, :], NT).astype(bf16).astype(f32) * 0.125).astype(bf16)
+        gt = _dot(wo2[...], gc[rows, :], NT).astype(bf16)
+        zt = jnp.concatenate([qt, gt], axis=0).astype(f32)
+        qt = jnp.concatenate([qt, none], axis=0)
+        gt = jnp.concatenate([none, gt], axis=0)
         return zt, qt, gt
 
     def scores(qt, part):
@@ -204,9 +202,7 @@
         att = (att * inv).astype(bf16).astype(f32)
         delta = jnp.sum(zt[DH:] * att, axis=0, keepdims=True)
         y = (zt * inv).T
-        yk = jnp.where(half, y, 0.0).astype(bf16)
-        yv = jnp.where(half, 0.0, y).astype(bf16)
-        ykv = jnp.concatenate([yk, yv], axis=0)
+        ykv = jnp.concatenate([jnp.where(half, y, 0.0), jnp.where(half, 0.0, y)], axis=0).astype(bf16)
         for part in parts:
             eb = eb_s[part, :]
             ds = (eb.astype(f32) * (dp_s[part, :] - delta)).astype(bf16)
@@ -281,8 +277,8 @@
             pltpu.VMEM((pad, E), bf16),
             pltpu.VMEM((LAT, 128), bf16),
             pltpu.VMEM((128, C), bf16),
-            pltpu.VMEM((128, E), bf16),
-            pltpu.VMEM((128, E), bf16),
+            pltpu.VMEM((DH, E), bf16),
+            pltpu.VMEM((DH, E), bf16),
             pltpu.VMEM((32, 128), jnp.int32),
             pltpu.VMEM((40, 128), jnp.int32),
             pltpu.SMEM((40, 128), jnp.int32),
@@ -315,26 +311,26 @@
     return t
 
 
-def head_kernel(parts, wk, wv, out, rest):
+def head_kernel(parts, wk, wv, out):
     dt = total_of(parts, slice(0, 128)).astype(bf16)
     for c in range(8):
         cols = slice(128 * c, 128 * (c + 1))
         w = jnp.concatenate([wk[:, cols], wv[:, cols]], axis=0)
         out[c] = _dot(dt, w, NN)
-    rest[...] = total_of(parts, slice(128, CHUNK))
 
 
 def run_head(parts, wk_t, wv_t):
     return pl.pallas_call(
         head_kernel,
-        out_shape=(pltpu.VMEM((8, 128, 128), f32), pltpu.VMEM((CHUNK - 128, 128), f32)),
+        out_shape=pltpu.VMEM((8, 128, 128), f32),
         in_specs=[VM] * 3,
-        out_specs=(VM,) * 2,
+        out_specs=VM,
         name="memory_part",
     )(in_vmem(parts), in_vmem(wk_t), in_vmem(wv_t))
 
 
-def weights_kernel(rest, gwq, gwk, gwv, gwo_t, scale_out):
+def weights_kernel(parts, gwq, gwk, gwv, gwo_t, scale_out):
+    rest = total_of(parts, slice(128, CHUNK))
     scale = 1.0 / rest[96:104, :]
     scale_out[...] = scale
     b = rest[0:96] * scale[0:1]
@@ -346,7 +342,7 @@
     gwo_t[...] = jnp.concatenate([qo_t[32:64], qo_t[96:128]], axis=1)
 
 
-def run_weights(rest):
+def run_weights(parts):
     small = jax.ShapeDtypeStruct((32, 64), f32)
     square = jax.ShapeDtypeStruct((64, 64), f32)
     return pl.pallas_call(
@@ -355,7 +351,7 @@
         in_specs=[VM],
         out_specs=(VM,) * 5,
         name="weight_parts",
-    )(in_vmem(rest))
+    )(in_vmem(parts))
 
 
 def last_kernel(parts, scale, gmem):
@@ -385,8 +381,8 @@
     )
     groups = [[z * 8 + x * 2 + core for z in range(2) for x in range(4)] for core in range(2)]
     parts = lax.all_to_all(keep + swap(send, "seq", 1), "seq", 0, 0, axis_index_groups=groups)
-    part, rest = run_head(parts, wk_t, wv_t)
-    grad_wq, grad_wk, grad_wv, grad_wo_t, scale = run_weights(rest)
+    part = run_head(parts, wk_t, wv_t)
+    grad_wq, grad_wk, grad_wv, grad_wo_t, scale = run_weights(parts)
     grad_memory = run_last(lax.all_to_all(part, "head", 0, 0), scale)
     return (grad_wq, grad_wk, grad_wv, grad_wo_t.T, grad_memory)
 

time: 61.8 us -> 61.3 us (level)
  no operation moved by 1% of the time
where the time goes in v6:
time: 61.3 us; the launch traced here: 60.7 us
  blocking collectives  29.6 us (48%)
  Pallas kernels  14.2 us (23%)
  waiting for transfers between devices  11.2 us (18%)
  starting transfers between devices  5 us (8%)
  between operations  0.68 us (1%)
    all_to_all x1, blocking collectives, shards(): lax.all_to_all(keep + swap(send, 'seq', 1), 'seq', 0, 0, axis_index_group...  29.6 us
    pallas_call x1, Pallas kernels, run_main(): pl.pallas_call(main_kernel, out_shape=(a, a), in_specs=[pl.BlockSpec(memo...  11.7 us
    all_to_all x1, waiting for transfers between devices, shards(): grad_memory = run_last(lax.all_to_all(part, 'head', 0, 0), scale)  8.68 us
    all_to_all x1, starting transfers between devices, shards(): grad_memory = run_last(lax.all_to_all(part, 'head', 0, 0), scale)  4.91 us
    ppermute x1, waiting for transfers between devices, swap(): return lax.ppermute(x, axis, [(i, i ^ bits) for i in range(n)])  2.51 us
  transfers between devices with their start and end apart: 2, of which 2 were waited for; matrix products, arithmetic and copies ran while one was open for 0% of the time, Pallas kernels for 1%

profile of v6, /device:TPU:0, one launch (start us, length us, event | category | flops | bytes accessed | tf_op | source)
XLA Modules:
  0.0 60.7 jit_solution(7458207294820745063)
XLA Ops:
  0.6 11.7 %masked_rows.1 = (f32[8,232,128]{2,1,0:T(8,128)S(1)}, f32[8,232,128]{2,1,0:T(8,128)S(1)}) custom-call(s32[1]{0:T(128)} %bitcast.sidx, s32[32,128]{1,0:T(8,128)} %bitcast.11, bf16[4096,512]{1,0:T(8,128)(2,1)} %q_hbm.1, bf16[4096,512]{1,0:T(8,128)(2,1)} %g_hbm.1, bf16[2048,1024]{1,0:T(8,128)(2,1)} %mem_hbm.1, bf16[64,512]{1,0:T(8,128)(2,1)} %bitcast.10, ...), custom_call_target="tpu_custom_call" | custom-call | flops 10000000000 | bytes 14680064 | tf_op jit(solution)/shard_map/masked_rows/pallas_call | solution.py:266
  12.4 0.0 copy-start
  12.4 0.0 copy-start.1
  12.4 0.1 collective-permute-start
  12.5 2.5 %collective-permute-done = f32[8,232,128]{2,1,0:T(8,128)S(1)} collective-permute-done((f32[8,232,128]{2,1,0:T(8,128)S(1)}, f32[8,232,128]{2,1,0:T(8,128)S(1)}, u32[]{:S(2)}, u32[]{:S(2)}) %collective-permute-start) | collective-permute-done | bytes 950304 | tf_op jit(solution)/shard_map/ppermute | solution.py:373
  15.0 0.1 add.3
  15.1 29.6 %all_to_all.10.parts = f32[8,232,128]{2,1,0:T(8,128)S(1)} all-to-all(f32[8,232,128]{2,1,0:T(8,128)S(1)} %add.3), channel_id=1, replica_groups={{0,16,32,48,64,80,96,112},{8,24,40,56,72,88,104,120},{1,17,33,49,65,81,..., dimensions={0} | all-to-all | bytes 1900544 | tf_op jit(solution)/shard_map/all_to_all | solution.py:383
  44.6 0.0 copy-done
  44.6 0.0 copy-done.1
  44.6 1.0 %memory_part.1 = f32[8,128,128]{2,1,0:T(8,128)} custom-call(f32[8,232,128]{2,1,0:T(8,128)S(1)} %all_to_all.10.parts, bf16[64,1024]{1,0:T(8,128)(2,1)S(1)} %bitcast.7, bf16[64,1024]{1,0:T(8,128)(2,1)S(1)} %bitcast.9), custom_call_target="tpu_custom_call" | custom-call | tf_op jit(solution)/shard_map/memory_part/pallas_call | solution.py:323
  45.7 4.9 %all-to-all-start.1 = ((f32[8,128,128]{2,1,0:T(8,128)}), f32[8,128,128]{2,1,0:T(8,128)S(1)}, u32[]{:S(2)}, u32[]{:S(2)}) async-start(f32[8,128,128]{2,1,0:T(8,128)} %memory_part.1), calls=%async_computation.1 | async-start | bytes 1048576 | tf_op jit(solution)/shard_map/all_to_all | solution.py:386
  50.6 0.8 %weight_parts.1 = (f32[32,64]{1,0:T(8,128)}, f32[64,64]{1,0:T(8,128)}, f32[64,64]{1,0:T(8,128)}, f32[32,64]{1,0:T(8,128)}, f32[8,128]{1,0:T(8,128)S(1)}) custom-call(f32[8,232,128]{2,1,0:T(8,128)S(1)} %all_to_all.10.parts), custom_call_target="tpu_custom_call" | custom-call | tf_op jit(solution)/shard_map/weight_parts/pallas_call | solution.py:348
  51.4 8.7 %all-to-all-done.1.parts = f32[8,128,128]{2,1,0:T(8,128)S(1)} async-done(((f32[8,128,128]{2,1,0:T(8,128)}), f32[8,128,128]{2,1,0:T(8,128)S(1)}, u32[]{:S(2)}, u32[]{:S(2)}) %all-to-all-start.1) | async-done | bytes 524320 | tf_op jit(solution)/shard_map/all_to_all | solution.py:386
  60.1 0.7 %grad_memory.1 = f32[128,128]{1,0:T(8,128)} custom-call(f32[8,128,128]{2,1,0:T(8,128)S(1)} %all-to-all-done.1.parts, f32[8,128]{1,0:T(8,128)S(1)} %get-tuple-element.18.scale), custom_call_target="tpu_custom_call" | custom-call | tf_op jit(solution)/shard_map/grad_memory/pallas_call | solution.py:362
Async XLA Ops:
  12.4 32.3 %copy-start = (bf16[1024,64]{0,1:T(8,128)(2,1)S(1)}, bf16[1024,64]{0,1:T(8,128)(2,1)}, u32[]{:S(2)}) copy-start(bf16[1024,64]{0,1:T(8,128)(2,1)} %param.11) | copy-start | bytes 393220
  12.4 32.3 %copy-start.1 = (bf16[1024,64]{0,1:T(8,128)(2,1)S(1)}, bf16[1024,64]{0,1:T(8,128)(2,1)}, u32[]{:S(2)}) copy-start(bf16[1024,64]{0,1:T(8,128)(2,1)} %param.12) | copy-start | bytes 393220
  12.4 2.6 %collective-permute-start = (f32[8,232,128]{2,1,0:T(8,128)S(1)}, f32[8,232,128]{2,1,0:T(8,128)S(1)}, u32[]{:S(2)}, u32[]{:S(2)}) collective-permute-start(f32[8,232,128]{2,1,0:T(8,128)S(1)} %get-tuple-element.13), channel_id=1, source_target_pairs={{0,8},{8,0},{16,24},{24,16},{32,40},{40,32},{48,56},{56,48},{64,72... | collective-permute-start | bytes 2850824 | tf_op jit(solution)/shard_map/ppermute | solution.py:373
  45.7 14.4 %all-to-all-start.1 = ((f32[8,128,128]{2,1,0:T(8,128)}), f32[8,128,128]{2,1,0:T(8,128)S(1)}, u32[]{:S(2)}, u32[]{:S(2)}) async-start(f32[8,128,128]{2,1,0:T(8,128)} %memory_part.1), calls=%async_computation.1 | async-start | bytes 1048576 | tf_op jit(solution)/shard_map/all_to_all | solution.py:386

commit v7 on v6

--- a/solution.py
+++ b/solution.py
@@ -16,7 +16,7 @@
 SMALL = 128
 LARGE = 272
 TB = 256
-CH = 256
+CH = 128
 ROW_PARTS = 4
 MEM_PARTS = 4
 CHUNK = 128 + 64 + 32 + 8

time: 61.3 us -> 62 us (1.011)
  no operation moved by 1% of the time
where the time goes in v7:
time: 62 us; the launch traced here: 61.4 us
  blocking collectives  30 us (48%)
  Pallas kernels  14.4 us (23%)
  waiting for transfers between devices  11.2 us (18%)
  starting transfers between devices  5 us (8%)
  between operations  0.68 us (1%)
    all_to_all x1, blocking collectives, shards(): lax.all_to_all(keep + swap(send, 'seq', 1), 'seq', 0, 0, axis_index_group...  30 us
    pallas_call x1, Pallas kernels, run_main(): pl.pallas_call(main_kernel, out_shape=(a, a), in_specs=[pl.BlockSpec(memo...  11.9 us
    all_to_all x1, waiting for transfers between devices, shards(): grad_memory = run_last(lax.all_to_all(part, 'head', 0, 0), scale)  8.68 us
    all_to_all x1, starting transfers between devices, shards(): grad_memory = run_last(lax.all_to_all(part, 'head', 0, 0), scale)  4.91 us
    ppermute x1, waiting for transfers between devices, swap(): return lax.ppermute(x, axis, [(i, i ^ bits) for i in range(n)])  2.51 us
  transfers between devices with their start and end apart: 2, of which 2 were waited for; matrix products, arithmetic and copies ran while one was open for 0% of the time, Pallas kernels for 1%

profile of v7, /device:TPU:0, one launch (start us, length us, event | category | flops | bytes accessed | tf_op | source)
XLA Modules:
  0.0 61.4 jit_solution(3485761602093403590)
XLA Ops:
  0.6 11.9 %masked_rows.1 = (f32[8,232,128]{2,1,0:T(8,128)S(1)}, f32[8,232,128]{2,1,0:T(8,128)S(1)}) custom-call(s32[1]{0:T(128)} %bitcast.sidx, s32[32,128]{1,0:T(8,128)} %bitcast.11, bf16[4096,512]{1,0:T(8,128)(2,1)} %q_hbm.1, bf16[4096,512]{1,0:T(8,128)(2,1)} %g_hbm.1, bf16[2048,1024]{1,0:T(8,128)(2,1)} %mem_hbm.1, bf16[64,512]{1,0:T(8,128)(2,1)} %bitcast.10, ...), custom_call_target="tpu_custom_call" | custom-call | flops 10000000000 | bytes 14680064 | tf_op jit(solution)/shard_map/masked_rows/pallas_call | solution.py:266
  12.6 0.0 copy-start
  12.6 0.0 copy-start.1
  12.6 0.1 collective-permute-start
  12.7 2.5 %collective-permute-done = f32[8,232,128]{2,1,0:T(8,128)S(1)} collective-permute-done((f32[8,232,128]{2,1,0:T(8,128)S(1)}, f32[8,232,128]{2,1,0:T(8,128)S(1)}, u32[]{:S(2)}, u32[]{:S(2)}) %collective-permute-start) | collective-permute-done | bytes 950304 | tf_op jit(solution)/shard_map/ppermute | solution.py:373
  15.2 0.1 add.3
  15.3 30.0 %all_to_all.10.parts = f32[8,232,128]{2,1,0:T(8,128)S(1)} all-to-all(f32[8,232,128]{2,1,0:T(8,128)S(1)} %add.3), channel_id=1, replica_groups={{0,16,32,48,64,80,96,112},{8,24,40,56,72,88,104,120},{1,17,33,49,65,81,..., dimensions={0} | all-to-all | bytes 1900544 | tf_op jit(solution)/shard_map/all_to_all | solution.py:383
  45.3 0.0 copy-done
  45.3 0.0 copy-done.1
  45.3 1.0 %memory_part.1 = f32[8,128,128]{2,1,0:T(8,128)} custom-call(f32[8,232,128]{2,1,0:T(8,128)S(1)} %all_to_all.10.parts, bf16[64,1024]{1,0:T(8,128)(2,1)S(1)} %bitcast.7, bf16[64,1024]{1,0:T(8,128)(2,1)S(1)} %bitcast.9), custom_call_target="tpu_custom_call" | custom-call | tf_op jit(solution)/shard_map/memory_part/pallas_call | solution.py:323
  46.4 4.9 %all-to-all-start.1 = ((f32[8,128,128]{2,1,0:T(8,128)}), f32[8,128,128]{2,1,0:T(8,128)S(1)}, u32[]{:S(2)}, u32[]{:S(2)}) async-start(f32[8,128,128]{2,1,0:T(8,128)} %memory_part.1), calls=%async_computation.1 | async-start | bytes 1048576 | tf_op jit(solution)/shard_map/all_to_all | solution.py:386
  51.3 0.8 %weight_parts.1 = (f32[32,64]{1,0:T(8,128)}, f32[64,64]{1,0:T(8,128)}, f32[64,64]{1,0:T(8,128)}, f32[32,64]{1,0:T(8,128)}, f32[8,128]{1,0:T(8,128)S(1)}) custom-call(f32[8,232,128]{2,1,0:T(8,128)S(1)} %all_to_all.10.parts), custom_call_target="tpu_custom_call" | custom-call | tf_op jit(solution)/shard_map/weight_parts/pallas_call | solution.py:348
  52.1 8.7 %all-to-all-done.1.parts = f32[8,128,128]{2,1,0:T(8,128)S(1)} async-done(((f32[8,128,128]{2,1,0:T(8,128)}), f32[8,128,128]{2,1,0:T(8,128)S(1)}, u32[]{:S(2)}, u32[]{:S(2)}) %all-to-all-start.1) | async-done | bytes 524320 | tf_op jit(solution)/shard_map/all_to_all | solution.py:386
  60.7 0.7 %grad_memory.1 = f32[128,128]{1,0:T(8,128)} custom-call(f32[8,128,128]{2,1,0:T(8,128)S(1)} %all-to-all-done.1.parts, f32[8,128]{1,0:T(8,128)S(1)} %get-tuple-element.18.scale), custom_call_target="tpu_custom_call" | custom-call | tf_op jit(solution)/shard_map/grad_memory/pallas_call | solution.py:362
Async XLA Ops:
  12.6 32.7 %copy-start = (bf16[1024,64]{0,1:T(8,128)(2,1)S(1)}, bf16[1024,64]{0,1:T(8,128)(2,1)}, u32[]{:S(2)}) copy-start(bf16[1024,64]{0,1:T(8,128)(2,1)} %param.11) | copy-start | bytes 393220
  12.6 32.7 %copy-start.1 = (bf16[1024,64]{0,1:T(8,128)(2,1)S(1)}, bf16[1024,64]{0,1:T(8,128)(2,1)}, u32[]{:S(2)}) copy-start(bf16[1024,64]{0,1:T(8,128)(2,1)} %param.12) | copy-start | bytes 393220
  12.6 2.6 %collective-permute-start = (f32[8,232,128]{2,1,0:T(8,128)S(1)}, f32[8,232,128]{2,1,0:T(8,128)S(1)}, u32[]{:S(2)}, u32[]{:S(2)}) collective-permute-start(f32[8,232,128]{2,1,0:T(8,128)S(1)} %get-tuple-element.13), channel_id=1, source_target_pairs={{0,8},{8,0},{16,24},{24,16},{32,40},{40,32},{48,56},{56,48},{64,72... | collective-permute-start | bytes 2850824 | tf_op jit(solution)/shard_map/ppermute | solution.py:373
  46.4 14.4 %all-to-all-start.1 = ((f32[8,128,128]{2,1,0:T(8,128)}), f32[8,128,128]{2,1,0:T(8,128)S(1)}, u32[]{:S(2)}, u32[]{:S(2)}) async-start(f32[8,128,128]{2,1,0:T(8,128)} %memory_part.1), calls=%async_computation.1 | async-start | bytes 1048576 | tf_op jit(solution)/shard_map/all_to_all | solution.py:386
